TPU v7x, 128 devices: a whole 4x4x4 slice. The times are simulated.
128 devices in a mesh: dp: 32 (over y, x, core), head: 4 (over z).
Axes of the slice: x: 4, y: 4, z: 4, core: 2. Of those that a mesh axis runs over, the one named last changes fastest.
Arguments:
- queries: bfloat16 [2048, 8192], P('dp', 'head'), as said below
- new_keys: bfloat16 [2048, 512], P('dp', 'head'), may hold values from -6 to 6
- new_values: bfloat16 [2048, 512], P('dp', 'head'), may hold values from -6 to 6
- key_cache: bfloat16 [2048, 4, 256, 128], P('dp', 'head'), may hold values from -6 to 6
- value_cache: bfloat16 [2048, 4, 256, 128], P('dp', 'head'), may hold values from -6 to 6
- cache_lengths: int32 [2048], P('dp'), may hold values from 1 to 256, as said below
- out_weight: bfloat16 [8192, 4096], P('head', 'dp'), may hold values from -0.0625 to 0.0625
- residual_in: bfloat16 [2048, 4096], P(('dp', 'head')), may hold values from -6 to 6
- norm_gain: float32 [4096], replicated, may hold values from 0.25 to 1.75
- expert_ids: int32 [2048, 8], P(('dp', 'head')), may hold values from 0 to 63, all different within a row; in each aligned block of 16 rows (0 to 15, 16 to 31, ...) at most 4 rows name the same one
- route_weights: float32 [2048, 8], P(('dp', 'head')), may hold values from 0.05 to 1
- w_gate: bfloat16 [64, 4096, 1536], P('dp', None, 'head'), may hold values from -0.09375 to 0.09375
- w_up: bfloat16 [64, 4096, 1536], P('dp', None, 'head'), may hold values from -0.09375 to 0.09375
- w_down: bfloat16 [64, 1536, 4096], P('dp', 'head'), may hold values from -0.15625 to 0.15625
Outputs:
- layer_out: bfloat16 [2048, 4096], P(('dp', 'head'))
Inputs may be any that keep to these rules, and one draw needn't show every extreme that they name: Each row's queries are real-valued; scores may be large. `cache_lengths`: at least one row in every draw has all 256 slots live. `expert_ids`: each row names 8 different experts; among the 16 rows of one device no expert is named by more than 4 rows.
All inputs are finite; a program needn't handle non-finite values.
Results may differ from a plain program's by a relative error of at most 0.0065.
Values may be sent and summed in bfloat16 or wider, within the bound.
A program may use at most 192 MiB of HBM per device.

v0:
```python
import math

import jax
import jax.numpy as jnp
from jax import lax
from jax.sharding import PartitionSpec as P


def attend(queries, new_keys, new_values, key_cache, value_cache, cache_lengths):
    row_count, kv_local, slot_count, head_size = key_cache.shape
    group = queries.shape[1] // (kv_local * head_size)
    factor = 1.0 / math.sqrt(head_size)
    block = math.gcd(128, slot_count)
    used = (jnp.max(cache_lengths) + block - 1) // block
    query = queries.reshape(row_count, kv_local, group, head_size)
    fresh = (
        jnp.einsum(
            "rjgd,rjd->rjg",
            query,
            new_keys.reshape(row_count, kv_local, head_size),
            preferred_element_type=jnp.float32,
        )
        * factor
    )

    def score_block(index, buffer):
        start = index * block
        keys = lax.dynamic_slice_in_dim(key_cache, start, block, 2)
        part_scores = (
            jnp.einsum("rjgd,rjtd->rjgt", query, keys, preferred_element_type=jnp.float32) * factor
        )
        return lax.dynamic_update_slice_in_dim(buffer, part_scores, start, 3)

    scores = lax.fori_loop(
        0, used, score_block, jnp.full((row_count, kv_local, group, slot_count), -1e30, jnp.float32)
    )
    live = jnp.arange(slot_count, dtype=jnp.int32)[None, :] < cache_lengths[:, None]
    scores = jnp.where(live[:, None, None, :], scores, -1e30)
    highest = jnp.maximum(jnp.max(scores, axis=-1), fresh)
    spread = jnp.exp(scores - highest[..., None])
    fresh_exp = jnp.exp(fresh - highest)
    denominator = jnp.sum(spread, axis=-1) + fresh_exp
    weights = (spread / denominator[..., None]).astype(jnp.bfloat16)
    fresh_weight = (fresh_exp / denominator).astype(jnp.bfloat16)

    def mix_block(index, total):
        start = index * block
        weight_part = lax.dynamic_slice_in_dim(weights, start, block, 3)
        values = lax.dynamic_slice_in_dim(value_cache, start, block, 2)
        return total + jnp.einsum(
            "rjgt,rjtd->rjgd", weight_part, values, preferred_element_type=jnp.float32
        )

    mixed = lax.fori_loop(
        0, used, mix_block, jnp.zeros((row_count, kv_local, group, head_size), jnp.float32)
    )
    mixed = mixed + fresh_weight.astype(jnp.float32)[..., None] * new_values.reshape(
        row_count, kv_local, 1, head_size
    ).astype(jnp.float32)
    return mixed.astype(jnp.bfloat16).reshape(row_count, kv_local * group * head_size)


def on_device(
    queries,
    new_keys,
    new_values,
    key_cache,
    value_cache,
    cache_lengths,
    out_weight,
    residual_in,
    norm_gain,
    expert_ids,
    route_weights,
    w_gate,
    w_up,
    w_down,
):
    dp_count = lax.axis_size("dp")
    head_count = lax.axis_size("head")
    attn = attend(queries, new_keys, new_values, key_cache, value_cache, cache_lengths)
    group_rows = attn.shape[0]
    feature_cols = out_weight.shape[1]
    share_rows = group_rows // head_count
    width = residual_in.shape[1]
    partial_proj = jnp.dot(
        lax.all_gather(attn, "dp", axis=0, tiled=True),
        out_weight,
        preferred_element_type=jnp.float32,
    )
    ordered = partial_proj.reshape(dp_count, head_count, share_rows, feature_cols).transpose(
        1, 0, 2, 3
    )
    ordered = ordered.reshape(head_count * dp_count * share_rows, feature_cols)
    summed_proj = lax.psum(ordered, "head")
    mine = lax.dynamic_slice_in_dim(
        summed_proj, lax.axis_index("head") * dp_count * share_rows, dp_count * share_rows, 0
    )
    proj = lax.all_to_all(mine, "dp", split_axis=0, concat_axis=1, tiled=True)
    hidden_one = residual_in.astype(jnp.float32) + proj
    normed = (
        hidden_one
        * lax.rsqrt(jnp.mean(hidden_one * hidden_one, axis=-1, keepdims=True) + 1e-06)
        * norm_gain
    ).astype(jnp.bfloat16)
    gates = route_weights / jnp.sum(route_weights, axis=-1, keepdims=True)
    experts_local = w_gate.shape[0]
    expert_count = experts_local * dp_count
    choose_count = expert_ids.shape[1]
    capacity = max(2, 2 * share_rows * choose_count // expert_count)
    flat = expert_ids.reshape(-1)
    onehot = (flat[:, None] == jnp.arange(expert_count, dtype=jnp.int32)[None, :]).astype(jnp.int32)
    earlier = jnp.cumsum(onehot, axis=0) - onehot
    position = jnp.sum(earlier * onehot, axis=1)
    target = flat * capacity + position
    places = jnp.arange(expert_count * capacity, dtype=jnp.int32)
    dispatch_mat = (target[None, :] == places[:, None]).astype(jnp.bfloat16)
    repeated = jnp.repeat(normed, choose_count, axis=0)
    outgoing = jnp.dot(dispatch_mat, repeated, preferred_element_type=jnp.float32).astype(
        jnp.bfloat16
    )
    outgoing = outgoing.reshape(dp_count, experts_local * capacity, width)
    arrived_rows = lax.all_to_all(outgoing, "dp", split_axis=0, concat_axis=0, tiled=True)
    shared = lax.all_gather(arrived_rows[None], "head", axis=0, tiled=True)
    tokens = shared.reshape(head_count * dp_count, experts_local * capacity, width)
    sources = tokens.shape[0]
    inputs = tokens.reshape(sources, experts_local, capacity, width)
    gate_val = jnp.einsum("secd,edf->secf", inputs, w_gate, preferred_element_type=jnp.float32)
    up_val = jnp.einsum("secd,edf->secf", inputs, w_up, preferred_element_type=jnp.float32)
    act = (jax.nn.silu(gate_val) * up_val).astype(jnp.bfloat16)
    result = jnp.einsum("secf,efd->secd", act, w_down, preferred_element_type=jnp.float32)
    result = result.reshape(sources, experts_local * capacity, width)
    result = result.reshape(head_count, dp_count, experts_local * capacity, width)
    summed_out = lax.psum_scatter(result, "head", scatter_dimension=0, tiled=True)
    returned = lax.all_to_all(summed_out[0], "dp", split_axis=0, concat_axis=0, tiled=True)
    returned = returned.reshape(expert_count * capacity, width)
    combine = jnp.sum(
        jnp.where(
            target.reshape(share_rows, choose_count)[:, :, None] == places[None, None, :],
            gates[:, :, None],
            jnp.zeros((), jnp.float32),
        ),
        axis=1,
    )
    moe_sum = jnp.dot(
        combine, returned, precision=lax.Precision.HIGHEST, preferred_element_type=jnp.float32
    )
    return (hidden_one + moe_sum).astype(jnp.bfloat16)


def solution(mesh):
    in_specs = (
        P("dp", "head"),
        P("dp", "head"),
        P("dp", "head"),
        P("dp", "head", None, None),
        P("dp", "head", None, None),
        P("dp"),
        P("head", "dp"),
        P(("dp", "head"), None),
        P(),
        P(("dp", "head"), None),
        P(("dp", "head"), None),
        P("dp", None, "head"),
        P("dp", None, "head"),
        P("dp", "head", None),
    )
    out_specs = P(("dp", "head"), None)
    return jax.shard_map(
        on_device, mesh=mesh, in_specs=in_specs, out_specs=out_specs, check_vma=False
    )
```

profile of v0, /device:TPU:0, one launch (start us, length us, event | category | flops | bytes accessed | tf_op | source)
XLA Modules:
  0.0 528.3 jit_solution(7997722237385152445)
XLA Ops:
  6.5 1.3 reduce_max.18
  8.5 0.7 iota_compare_fusion.4
  9.3 1.0 copy.54
  10.5 5.6 %while.20 = (s32[]{:T(128)}, f32[64,1,16,256]{3,2,0,1:T(8,128)S(1)}, s32[]{:T(128)}, bf16[64,1,256,128]{3,2,0,1:T(8,128)(2,1)}, bf16[64,1,16,128]{3,2,0,1:T(8,12...) while((s32[]{:T(128)}, f32[64,1,16,256]{3,2,0,1:T(8,128)S(1)}, s32[]{:T(128)}, ...), condition=%wide.region_2.3_spmd, body=%wide.region_1.2_spmd.sunk | while | flops 33685508 | bytes 2884747 | solution.py:34
  10.5 2.8 fusion.69
  13.3 2.8 fusion.69
  16.3 0.2 fusion.46
  16.6 0.5 fusion.42
  17.1 0.4 divide_convert_fusion
  17.5 4.6 while.21
  17.5 2.3 fusion.72
  19.8 2.3 fusion.72
  22.3 0.8 copy.67
  23.2 55.3 %all-gather.4.cloned.1.call-done = bf16[2048,2048]{1,0:T(8,128)(2,1)} async-done(((bf16[64,2048]{1,0:T(8,128)(2,1)}), bf16[2048,2048]{1,0:T(8,128)(2,1)}) %all-gather.4.cloned.1.call-update) | async-done | bytes 8388624 | tf_op jit(solution)/shard_map/all_gather | solution.py:87
  78.5 5.8 %fusion.50 = f32[2048,128]{1,0:T(8,128)S(1)} fusion(bf16[2048,2048]{1,0:T(8,128)(2,1)} %all-gather.4.cloned.1.call-done, bf16[2048,128]{1,0:T(8,128)(2,1)S(1)} %copy-done), kind=kOutput, calls=%fused_computation.65 | convolution fusion | flops 1073741824 | bytes 9961472 | tf_op jit(solution)/shard_map/dot_general | solution.py:86
  84.3 1.1 copy.41
  85.9 45.5 %all-reduce.2.cloned.1.call-done = f32[2048,128]{1,0:T(8,128)} async-done(((f32[2048,128]{1,0:T(8,128)}), f32[2048,128]{1,0:T(8,128)}) %all-reduce.2.cloned.1.call-update) | async-done | bytes 1048592 | tf_op jit(solution)/shard_map/psum | solution.py:95
  131.3 1.7 constant_dynamic-slice_fusion
  133.0 7.0 %all-to-all-start = ((f32[32,16,128]{2,1,0:T(8,128)}), f32[32,16,128]{2,1,0:T(8,128)S(1)}, u32[]{:S(2)}, u32[]{:S(2)}) async-start(f32[32,16,128]{2,1,0:T(8,128)} %bitcast.15), calls=%async_computation | async-start | bytes 524288 | tf_op jit(solution)/shard_map/all_to_all | solution.py:99
  140.2 8.7 %all-to-all-done = f32[32,16,128]{2,1,0:T(8,128)S(1)} async-done(((f32[32,16,128]{2,1,0:T(8,128)}), f32[32,16,128]{2,1,0:T(8,128)S(1)}, u32[]{:S(2)}, u32[]{:S(2)}) %all-to-all-start) | async-done | bytes 262176 | tf_op jit(solution)/shard_map/all_to_all | solution.py:99
  149.2 0.7 fusion.32
  149.9 32.3 %all_to_all.29 = bf16[32,8,4096]{2,1,0:T(8,128)(2,1)} all-to-all(bf16[32,8,4096]{2,1,0:T(8,128)(2,1)S(1)} %fusion.32), channel_id=1, replica_groups=mesh['dp'=32,'head'=4] {'dp'}, dimensions={0} | all-to-all | bytes 4194304 | tf_op jit(solution)/shard_map/all_to_all | solution.py:123
  182.4 80.4 %all-gather.6.cloned.1.call-done = bf16[128,8,4096]{2,1,0:T(8,128)(2,1)} async-done(((bf16[32,8,4096]{2,1,0:T(8,128)(2,1)}), bf16[128,8,4096]{2,1,0:T(8,128)(2,1)}) %all-gather.6.cloned.1.call-update) | async-done | bytes 8388624 | tf_op jit(solution)/shard_map/all_gather | solution.py:124
  262.8 11.2 %copy.46 = bf16[128,8,4096]{2,0,1:T(8,128)(2,1)} copy(bf16[128,8,4096]{2,1,0:T(8,128)(2,1)} %all-gather.6.cloned.1.call-done) | data formatting | bytes 16777216 | tf_op jit(solution)/shard_map/all_gather | solution.py:124
  274.0 9.1 %fusion.30 = f32[2,128,4,384]{3,1,2,0:T(8,128)S(1)} fusion(bf16[128,2,4,4096]{3,0,2,1:T(8,128)(2,1)} %bitcast.141, bf16[2,4096,384]{2,1,0:T(8,128)(2,1)} %param.29), kind=kOutput, calls=%fused_computation.20 | convolution fusion | flops 3221225472 | bytes 16252928 | tf_op jit(solution)/shard_map/secd,edf->secf/dot_general | solution.py:128
  283.1 7.5 %fusion.35 = bf16[128,2,4,384]{3,0,2,1:T(8,128)(2,1)S(1)} fusion(f32[2,128,4,384]{3,1,2,0:T(8,128)S(1)} %fusion.30, bf16[128,2,4,4096]{3,0,2,1:T(8,128)(2,1)S(1)} %bitcast.142, bf16[2,4096,384]{2,1,0:T(8,128)(2,1)} %param.30), kind=kOutput, calls=%fused_computation.28 | convolution fusion | flops 3223584768 | bytes 17039360 | tf_op jit(solution)/shard_map/secd,edf->secf/dot_general | solution.py:129
  290.7 4.5 fusion.26
  295.2 11.7 %copy.47 = f32[4,32,8,4096]{3,2,1,0:T(8,128)} copy(f32[4,32,8,4096]{3,1,0,2:T(8,128)S(1)} %bitcast.136) | data formatting | bytes 33554432 | tf_op jit(solution)/shard_map/reshape;reshape | solution.py:133
  306.9 149.1 %reduce-scatter.2.cloned.1.call-done = f32[1,32,8,4096]{3,2,1,0:T(8,128)} async-done(((f32[4,32,8,4096]{3,2,1,0:T(8,128)}), f32[1,32,8,4096]{3,2,1,0:T(8,128)}) %reduce-scatter.2.cloned.1.call-update) | async-done | bytes 4194320 | tf_op jit(solution)/shard_map/reduce_scatter | solution.py:134
  456.0 7.4 %all-to-all-start.2 = ((f32[32,8,4096]{2,1,0:T(8,128)}), f32[32,8,4096]{2,1,0:T(8,128)}, u32[]{:S(2)}, u32[]{:S(2)}) async-start(f32[32,8,4096]{2,1,0:T(8,128)} %bitcast.145), calls=%async_computation.3 | async-start | bytes 8388608 | tf_op jit(solution)/shard_map/all_to_all | solution.py:135
  463.8 53.1 %all-to-all-done.2 = f32[32,8,4096]{2,1,0:T(8,128)} async-done(((f32[32,8,4096]{2,1,0:T(8,128)}), f32[32,8,4096]{2,1,0:T(8,128)}, u32[]{:S(2)}, u32[]{:S(2)}) %all-to-all-start.2) | async-done | bytes 4194336 | tf_op jit(solution)/shard_map/all_to_all | solution.py:135
  516.9 4.9 fusion.33
  (53 shorter events, 2.2 us)
Async XLA Ops:
  6.5 72.0 %copy-start = (bf16[2048,128]{1,0:T(8,128)(2,1)S(1)}, bf16[2048,128]{1,0:T(8,128)(2,1)}, u32[]{:S(2)}) copy-start(bf16[2048,128]{1,0:T(8,128)(2,1)} %param.24) | copy-start | bytes 1572868
  6.5 71.9 %all-gather.4.cloned.1.call-start = ((), (), s32[]{:S(2)}) async-start(), calls=%async_computation.4 | async-start | bytes 8650752 | tf_op jit(solution)/shard_map/all_gather | solution.py:87
  10.4 5.9 %copy-start.8 = (bf16[64,128]{1,0:T(8,128)(2,1)S(1)}, bf16[64,128]{1,0:T(8,128)(2,1)}, u32[]{:S(2)}) copy-start(bf16[64,128]{1,0:T(8,128)(2,1)} %param.19) | copy-start | bytes 49156
  17.5 4.6 copy-start.4
  23.1 62.3 %copy-start.7 = (s32[16,8]{0,1:T(8,128)S(1)}, s32[16,8]{0,1:T(8,128)}, u32[]{:S(2)}) copy-start(s32[16,8]{0,1:T(8,128)} %param.27) | copy-start | bytes 1540
  23.1 108.2 %all-reduce.2.cloned.1.call-start = ((), (), s32[]{:S(2)}) async-start(), calls=%async_computation.5 | async-start | bytes 2097152 | tf_op jit(solution)/shard_map/psum | solution.py:95
  84.3 64.6 %copy-start.3 = (bf16[16,4096]{1,0:T(8,128)(2,1)S(1)}, bf16[16,4096]{1,0:T(8,128)(2,1)}, u32[]{:S(2)}) copy-start(bf16[16,4096]{1,0:T(8,128)(2,1)} %param.25) | copy-start | bytes 393220
  84.3 64.8 %copy-start.5 = (f32[4096]{0:T(1024)S(1)}, f32[4096]{0:T(1024)}, u32[]{:S(2)}) copy-start(f32[4096]{0:T(1024)} %param.26) | copy-start | bytes 49156
  133.0 15.9 %all-to-all-start = ((f32[32,16,128]{2,1,0:T(8,128)}), f32[32,16,128]{2,1,0:T(8,128)S(1)}, u32[]{:S(2)}, u32[]{:S(2)}) async-start(f32[32,16,128]{2,1,0:T(8,128)} %bitcast.15), calls=%async_computation | async-start | bytes 524288 | tf_op jit(solution)/shard_map/all_to_all | solution.py:99
  140.0 122.8 %all-gather.6.cloned.1.call-start = ((), (), s32[]{:S(2)}) async-start(), calls=%async_computation.7 | async-start | bytes 10485760 | tf_op jit(solution)/shard_map/all_gather | solution.py:124
  182.2 273.9 %reduce-scatter.2.cloned.1.call-start = ((), (), s32[]{:S(2)}) async-start(), calls=%async_computation.6 | async-start | bytes 20971520 | tf_op jit(solution)/shard_map/reduce_scatter | solution.py:134
  274.0 9.1 %copy-start.2 = (bf16[128,8,4096]{2,0,1:T(8,128)(2,1)S(1)}, bf16[128,8,4096]{2,0,1:T(8,128)(2,1)}, u32[]{:S(2)}) copy-start(bf16[128,8,4096]{2,0,1:T(8,128)(2,1)} %copy.46) | copy-start | bytes 25165828
  274.0 16.6 %slice-start = ((s8[6291456]{0:T(1024)(128)(4,1)}), s8[4194304]{0:T(1024)(128)(4,1)S(1)}, s32[]{:S(2)}) async-start(s8[6291456]{0:T(1024)(128)(4,1)} %bitcast.143), calls=%async_computation.8 | async-start | bytes 8388608
  283.1 7.5 %slice-start.1 = ((s8[6291456]{0:T(1024)(128)(4,1)}), s8[2097152]{0:T(1024)(128)(4,1)S(1)}, s32[]{:S(2)}) async-start(s8[6291456]{0:T(1024)(128)(4,1)} %bitcast.143), calls=%async_computation.9 | async-start | bytes 4194304
  456.0 7.5 %copy-start.6 = (f32[16,8]{0,1:T(8,128)S(1)}, f32[16,8]{0,1:T(8,128)}, u32[]{:S(2)}) copy-start(f32[16,8]{0,1:T(8,128)} %param.28) | copy-start | bytes 1540
  456.0 60.8 %all-to-all-start.2 = ((f32[32,8,4096]{2,1,0:T(8,128)}), f32[32,8,4096]{2,1,0:T(8,128)}, u32[]{:S(2)}, u32[]{:S(2)}) async-start(f32[32,8,4096]{2,1,0:T(8,128)} %bitcast.145), calls=%async_computation.3 | async-start | bytes 8388608 | tf_op jit(solution)/shard_map/all_to_all | solution.py:135
  463.4 58.4 %copy-start.1 = (bf16[2048,128]{1,0:T(8,128)(2,1)S(1)}, bf16[2048,128]{1,0:T(8,128)(2,1)}, u32[]{:S(2)}) copy-start(bf16[2048,128]{1,0:T(8,128)(2,1)} %param.24) | copy-start | bytes 1572868
Sparse Core Ops, SparseCore 0:
  23.2 55.2 all-gather.3
  85.5 45.7 all-reduce.1
  182.3 80.5 all-gather.5
  307.1 148.9 reduce-scatter.1
where the time goes:
time: 529 us; the launch traced here: 528 us
  waiting for transfers between devices  392 us (74%)
  matrix products  42.8 us (8%)
  blocking collectives  32.3 us (6%)
  local copies, waits for them, and re-layouts  28 us (5%)
  starting transfers between devices  14.6 us (3%)
  between operations  14.1 us (3%)
    reduce_scatter x1, waiting for transfers between devices, on_device(): lax.psum_scatter(result, 'head', scatter_dimension=0, tiled=True)  149 us
    all_gather x1, waiting for transfers between devices, on_device(): shared = lax.all_gather(arrived_rows[None], 'head', axis=0, tiled=True)  80.4 us
    all_gather x1, waiting for transfers between devices, on_device(): lax.all_gather(attn, 'dp', axis=0, tiled=True)  55.3 us
    all_to_all x1, waiting for transfers between devices, on_device(): lax.all_to_all(summed_out[0], 'dp', split_axis=0, concat_axis=0, tiled=True)  53.1 us
    psum x1, waiting for transfers between devices, on_device(): summed_proj = lax.psum(ordered, 'head')  45.5 us
    all_to_all x1, blocking collectives, on_device(): lax.all_to_all(outgoing, 'dp', split_axis=0, concat_axis=0, tiled=True)  32.3 us
    another operation x1, local copies, waits for them, and re-layouts, on_device(): result.reshape(head_count, dp_count, experts_local * capacity, width)  11.7 us
    all_gather x1, local copies, waits for them, and re-layouts, on_device(): shared = lax.all_gather(arrived_rows[None], 'head', axis=0, tiled=True)  11.2 us
  transfers between devices with their start and end apart: 6, of which 6 were waited for; matrix products, arithmetic and copies ran while one was open for 0% of the time, Pallas kernels for 0%

commit v1 on v0

--- a/solution.py
+++ b/solution.py
@@ -3,7 +3,313 @@
 import jax
 import jax.numpy as jnp
 from jax import lax
+from jax.experimental import pallas as pl
+from jax.experimental.pallas import tpu as pltpu
 from jax.sharding import PartitionSpec as P
+
+MESH = pl.DeviceIdType.MESH
+SIDE = 4
+WIDTH = 4096
+BLOCK = 16
+CAPACITY = 4
+PARTS = (
+    ("x", "y", "z", 0, 1408),
+    ("y", "z", "x", 1408, 1408),
+    ("z", "x", "y", 2816, 1280),
+)
+
+
+def my_place():
+    row = lax.axis_index("dp")
+    return {
+        "y": row // (2 * SIDE),
+        "x": (row // 2) % SIDE,
+        "c": row % 2,
+        "z": lax.axis_index("head"),
+    }
+
+
+def device_of(place):
+    return ((place["y"] * SIDE + place["x"]) * 2 + place["c"], place["z"])
+
+
+def shifted(place, axis, by):
+    other = dict(place)
+    other[axis] = (place[axis] + by) % SIDE
+    return other
+
+
+def sibling_of(place):
+    other = dict(place)
+    other["c"] = 1 - place["c"]
+    return other
+
+
+def greet(partners):
+    barrier = pltpu.get_barrier_semaphore()
+    for partner in partners:
+        pl.semaphore_signal(barrier, inc=1, device_id=device_of(partner), device_id_type=MESH)
+    pl.semaphore_wait(barrier, len(partners))
+
+
+def remote(src, dst, send, recv, place):
+    return pltpu.make_async_remote_copy(
+        src_ref=src, dst_ref=dst, send_sem=send, recv_sem=recv,
+        device_id=device_of(place), device_id_type=MESH,
+    )
+
+
+def blocks_at(ref, core, place, free, halves, columns):
+    index = [core]
+    last = max(free, key="zyx".index, default=None)
+    for axis in ("z", "y", "x"):
+        if axis in free:
+            if halves is not None and axis == last:
+                index.append(pl.ds(halves * (SIDE // 2), SIDE // 2))
+            else:
+                index.append(slice(None))
+        else:
+            index.append(place[axis])
+    start, size = columns
+    if not free and halves is not None:
+        low = (size // 256) * 128
+        start, size = (start, low) if halves == 0 else (start + low, size - low)
+    return ref.at[(*index, slice(None), pl.ds(start, size))]
+
+
+def gather_kernel(mine_ref, all_ref, own_sem, near_send, near_recv, far_send, far_recv, pair_send, pair_recv, first_send, first_recv):
+    me = my_place()
+    core = me["c"]
+    sibling = sibling_of(me)
+    greet([sibling] + [shifted(me, axis, by) for axis in "xyz" for by in (1, -1)])
+    home = all_ref.at[core, me["z"], me["y"], me["x"]]
+    own = pltpu.make_async_copy(mine_ref, home, own_sem)
+    own.start()
+    first = remote(mine_ref, home, first_send, first_recv, sibling)
+    first.start()
+    own.wait()
+    waits = [first]
+
+    def group(part, stage, coordinate_shift, halves=None):
+        order, start, size = PARTS[part][:3], PARTS[part][3], PARTS[part][4]
+        place = shifted(me, order[stage], coordinate_shift)
+        return blocks_at(all_ref, core, place, order[:stage], halves, (start, size))
+
+    def to_pair(part, stage, number, block):
+        copy = remote(block, block, pair_send.at[part, stage, number], pair_recv.at[part, stage, number], sibling)
+        copy.start()
+        waits.append(copy)
+
+    for stage in range(3):
+        near = {}
+        for part in range(3):
+            axis = PARTS[part][stage]
+            block = group(part, stage, 0)
+            for way, by in ((0, 1), (1, -1)):
+                copy = remote(block, block, near_send.at[part, stage, way], near_recv.at[part, stage, way], shifted(me, axis, by))
+                copy.start()
+                near[part, way] = copy
+        far = {}
+        for part in range(3):
+            axis = PARTS[part][stage]
+            for way, by in ((0, 1), (1, -1)):
+                near[part, way].wait_recv()
+                block = group(part, stage, -by, way)
+                copy = remote(block, block, far_send.at[part, stage, way], far_recv.at[part, stage, way], shifted(me, axis, by))
+                copy.start()
+                far[part, way] = copy
+                to_pair(part, stage, way, group(part, stage, -by))
+        for part in range(3):
+            for way in (0, 1):
+                far[part, way].wait_recv()
+            to_pair(part, stage, 2, group(part, stage, 2))
+        for part in range(3):
+            for way in (0, 1):
+                near[part, way].wait_send()
+                far[part, way].wait_send()
+    for copy in waits:
+        copy.wait()
+
+
+def gather_rows(mine):
+    return pl.pallas_call(
+        gather_kernel,
+        out_shape=jax.ShapeDtypeStruct((2, SIDE, SIDE, SIDE, BLOCK, WIDTH), jnp.bfloat16),
+        in_specs=[pl.BlockSpec(memory_space=pl.ANY)],
+        out_specs=pl.BlockSpec(memory_space=pl.ANY),
+        scratch_shapes=[
+            pltpu.SemaphoreType.DMA,
+            pltpu.SemaphoreType.DMA((3, 3, 2)),
+            pltpu.SemaphoreType.DMA((3, 3, 2)),
+            pltpu.SemaphoreType.DMA((3, 3, 2)),
+            pltpu.SemaphoreType.DMA((3, 3, 2)),
+            pltpu.SemaphoreType.DMA((3, 3, 3)),
+            pltpu.SemaphoreType.DMA((3, 3, 3)),
+            pltpu.SemaphoreType.DMA,
+            pltpu.SemaphoreType.DMA,
+        ],
+        compiler_params=pltpu.CompilerParams(collective_id=1, has_side_effects=True),
+    )(mine)
+
+
+def reduce_kernel(parts_ref, base_ref, out_ref, acc, pair_buf, near1, near2, near3, far1, far2, far3,
+                  local_sem, pair_send, pair_recv, near_send, near_recv, far_send, far_recv):
+    me = my_place()
+    core = me["c"]
+    sibling = sibling_of(me)
+    near_bufs, far_bufs = (near1, near2, near3), (far1, far2, far3)
+    greet([sibling] + [shifted(me, axis, by) for axis in "xyz" for by in (1, -1)])
+    waits = []
+
+    def axis_of(part, stage):
+        return PARTS[part][2 - stage]
+
+    def free_of(part, stage):
+        return PARTS[part][: 2 - stage]
+
+    def columns_of(part):
+        return PARTS[part][3], PARTS[part][4]
+
+    def group(ref, part, stage, shift, which, halves=None):
+        place = shifted(me, axis_of(part, stage), shift)
+        return blocks_at(ref, which, place, free_of(part, stage), halves, columns_of(part))
+
+    shifts = (2, 1, -1, 0)
+    pair, local = {}, {}
+    for number, shift in enumerate(shifts):
+        for part in range(3):
+            copy = remote(
+                group(parts_ref, part, 0, shift, 1 - core),
+                group(pair_buf, part, 0, shift, 0),
+                pair_send.at[part, number], pair_recv.at[part, number], sibling,
+            )
+            copy.start()
+            pair[part, number] = copy
+            waits.append(copy)
+            copy = pltpu.make_async_copy(group(parts_ref, part, 0, shift, core), group(acc, part, 0, shift, 0), local_sem.at[part, number])
+            copy.start()
+            local[part, number] = copy
+
+    def add_into(target, others):
+        lead = target.shape[:-2]
+        count = 1
+        for size in lead:
+            count *= size
+
+        def body(at, _):
+            index = []
+            rest = at
+            for size in reversed(lead):
+                index.insert(0, rest % size)
+                rest = rest // size
+            index = (*index, slice(None), slice(None))
+            total = target[index].astype(jnp.float32)
+            for other in others:
+                total += other[index].astype(jnp.float32)
+            target[index] = total.astype(target.dtype)
+            return 0
+
+        if count == 1:
+            body(0, 0)
+        else:
+            lax.fori_loop(0, count, body, 0)
+
+    for stage in range(3):
+        near, far = {}, {}
+
+        def far_copy(part, way):
+            axis = axis_of(part, stage)
+            by = 1 if way == 0 else -1
+            src = group(acc, part, stage, 2, 0, way)
+            dst = far_bufs[stage].at[part, way, ..., pl.ds(0, src.shape[-1])]
+            return remote(src, dst,
+                          far_send.at[part, stage, way], far_recv.at[part, stage, way], shifted(me, axis, by))
+
+        def near_copy(part, way, half):
+            axis = axis_of(part, stage)
+            by = 1 if way == 0 else -1
+            src = group(acc, part, stage, by, 0, half)
+            dst = near_bufs[stage].at[part, way, half, ..., pl.ds(0, src.shape[-1])]
+            return remote(src, dst, near_send.at[part, stage, way, half], near_recv.at[part, stage, way, half], shifted(me, axis, by))
+
+        for part in range(3):
+            if stage == 0:
+                local[part, 0].wait()
+                pair[part, 0].wait_recv()
+                add_into(group(acc, part, 0, 2, 0), [group(pair_buf, part, 0, 2, 0)])
+            for way in (0, 1):
+                far[part, way] = far_copy(part, way)
+                far[part, way].start()
+        for part in range(3):
+            for way, by in ((0, 1), (1, -1)):
+                if stage == 0:
+                    local[part, 1 + way].wait()
+                    pair[part, 1 + way].wait_recv()
+                    add_into(group(acc, part, 0, by, 0), [group(pair_buf, part, 0, by, 0)])
+                near[part, way, 1 - way] = near_copy(part, way, 1 - way)
+                near[part, way, 1 - way].start()
+        for part in range(3):
+            for way, by in ((0, 1), (1, -1)):
+                far[part, way].wait_recv()
+                target = group(acc, part, stage, by, 0, way)
+                add_into(target, [far_bufs[stage].at[part, way, ..., pl.ds(0, target.shape[-1])]])
+                near[part, way, way] = near_copy(part, way, way)
+                near[part, way, way].start()
+        for part in range(3):
+            if stage == 0:
+                local[part, 3].wait()
+                pair[part, 3].wait_recv()
+                add_into(group(acc, part, 0, 0, 0), [group(pair_buf, part, 0, 0, 0)])
+        for part in range(3):
+            for half in (0, 1):
+                for way in (0, 1):
+                    near[part, way, half].wait_recv()
+                target = group(acc, part, stage, 0, 0, half)
+                others = [near_bufs[stage].at[part, way, half, ..., pl.ds(0, target.shape[-1])] for way in (0, 1)]
+                if stage < 2:
+                    add_into(target, others)
+                else:
+                    total = target[...].astype(jnp.float32)
+                    for other in others:
+                        total += other[...].astype(jnp.float32)
+                    start, size = columns_of(part)
+                    low = (size // 256) * 128
+                    start, size = (start, low) if half == 0 else (start + low, size - low)
+                    out_ref[:, pl.ds(start, size)] = (base_ref[:, pl.ds(start, size)] + total).astype(out_ref.dtype)
+        for copy in [*near.values(), *far.values()]:
+            copy.wait_send()
+    for copy in waits:
+        copy.wait_send()
+
+
+def reduce_rows(parts, base):
+    wide = 1408
+    half = SIDE // 2
+    vmem = pl.BlockSpec(memory_space=pltpu.VMEM)
+    return pl.pallas_call(
+        reduce_kernel,
+        out_shape=jax.ShapeDtypeStruct((BLOCK, WIDTH), jnp.bfloat16),
+        in_specs=[pl.BlockSpec(memory_space=pl.ANY), vmem],
+        out_specs=vmem,
+        scratch_shapes=[
+            pltpu.VMEM((1, SIDE, SIDE, SIDE, BLOCK, WIDTH), jnp.bfloat16),
+            pltpu.VMEM((1, SIDE, SIDE, SIDE, BLOCK, WIDTH), jnp.bfloat16),
+            pltpu.VMEM((3, 2, 2, SIDE, half, BLOCK, wide), jnp.bfloat16),
+            pltpu.VMEM((3, 2, 2, half, BLOCK, wide), jnp.bfloat16),
+            pltpu.VMEM((3, 2, 2, BLOCK, wide // 2 + 64), jnp.bfloat16),
+            pltpu.VMEM((3, 2, SIDE, half, BLOCK, wide), jnp.bfloat16),
+            pltpu.VMEM((3, 2, half, BLOCK, wide), jnp.bfloat16),
+            pltpu.VMEM((3, 2, BLOCK, wide // 2 + 64), jnp.bfloat16),
+            pltpu.SemaphoreType.DMA((3, 4)),
+            pltpu.SemaphoreType.DMA((3, 4)),
+            pltpu.SemaphoreType.DMA((3, 4)),
+            pltpu.SemaphoreType.DMA((3, 3, 2, 2)),
+            pltpu.SemaphoreType.DMA((3, 3, 2, 2)),
+            pltpu.SemaphoreType.DMA((3, 3, 2)),
+            pltpu.SemaphoreType.DMA((3, 3, 2)),
+        ],
+        compiler_params=pltpu.CompilerParams(collective_id=2, has_side_effects=True, vmem_limit_bytes=60 * 1024 * 1024),
+    )(parts, base)
 
 
 def attend(queries, new_keys, new_values, key_cache, value_cache, cache_lengths):
@@ -58,6 +364,47 @@
         row_count, kv_local, 1, head_size
     ).astype(jnp.float32)
     return mixed.astype(jnp.bfloat16).reshape(row_count, kv_local * group * head_size)
+
+
+def route_codes(expert_ids, route_weights):
+    gates = route_weights / jnp.sum(route_weights, axis=-1, keepdims=True)
+    rows = expert_ids.shape[0]
+    same = jnp.any(expert_ids[:, :, None, None] == expert_ids[None, None, :, :], axis=-1)
+    earlier = jnp.arange(rows)[None, None, :] < jnp.arange(rows)[:, None, None]
+    position = jnp.sum((same & earlier).astype(jnp.int32), axis=-1)
+    codes = (expert_ids * CAPACITY + position).astype(jnp.float32)
+    return jnp.stack([codes.T.reshape(-1), gates.T.reshape(-1)])
+
+
+def experts(rows, codes, w_gate, w_up, w_down):
+    groups, span = 8, 256
+    tokens = rows.reshape(groups, span, WIDTH)
+    choices = codes.shape[-1] // BLOCK
+    table = codes.reshape(SIDE, SIDE, 2, SIDE, 2, choices, BLOCK)
+    table = table.transpose(4, 5, 2, 3, 0, 1, 6).reshape(2, choices, groups, span // BLOCK, BLOCK)
+    first = (lax.axis_index("dp") * 2 * CAPACITY).astype(jnp.float32)
+    place = jnp.arange(span // BLOCK, dtype=jnp.float32)[None, :, None] * CAPACITY
+    slots, weights = [], []
+    for own in range(2):
+        code = table[0] - (first + own * CAPACITY)
+        hit = (code >= 0) & (code < CAPACITY)
+        slot = jnp.sum(jnp.where(hit, code + 1, 0.0), axis=0)
+        slots.append(jnp.where(slot > 0, slot - 1 + place + own * 64, -1.0).reshape(groups, span))
+        weights.append(jnp.sum(jnp.where(hit, table[1], 0.0), axis=0).reshape(groups, span))
+    spot = jnp.arange(128, dtype=jnp.float32)[None, :, None]
+    picks = [spot == slot[:, None, :] for slot in slots]
+    pick = (picks[0] | picks[1]).astype(jnp.bfloat16)
+    scale = jnp.sum(jnp.where(picks[0], weights[0][:, None, :], 0.0) + jnp.where(picks[1], weights[1][:, None, :], 0.0), axis=-1)
+    chosen = jnp.einsum("gsr,grd->gsd", pick, tokens, preferred_element_type=jnp.float32).astype(jnp.bfloat16)
+    chosen = chosen.reshape(groups, 2, 64, WIDTH)
+    scale = scale.reshape(groups, 2, 64)
+    gate_val = jnp.einsum("gesd,edf->gesf", chosen, w_gate, preferred_element_type=jnp.float32)
+    up_val = jnp.einsum("gesd,edf->gesf", chosen, w_up, preferred_element_type=jnp.float32)
+    act = (jax.nn.silu(gate_val) * up_val * scale[..., None]).astype(jnp.bfloat16)
+    result = jnp.einsum("gesf,efd->gesd", act, w_down, preferred_element_type=jnp.float32).astype(jnp.bfloat16)
+    result = result.reshape(groups, 128, WIDTH)
+    spread = jnp.einsum("gsr,gsd->grd", pick, result, preferred_element_type=jnp.float32).astype(jnp.bfloat16)
+    return spread.reshape(2, SIDE, SIDE, SIDE, BLOCK, WIDTH)
 
 
 def on_device(
@@ -78,6 +425,7 @@
 ):
     dp_count = lax.axis_size("dp")
     head_count = lax.axis_size("head")
+    codes = lax.all_gather(route_codes(expert_ids, route_weights), ("dp", "head"), axis=0, tiled=False)
     attn = attend(queries, new_keys, new_values, key_cache, value_cache, cache_lengths)
     group_rows = attn.shape[0]
     feature_cols = out_weight.shape[1]
@@ -103,49 +451,9 @@
         * lax.rsqrt(jnp.mean(hidden_one * hidden_one, axis=-1, keepdims=True) + 1e-06)
         * norm_gain
     ).astype(jnp.bfloat16)
-    gates = route_weights / jnp.sum(route_weights, axis=-1, keepdims=True)
-    experts_local = w_gate.shape[0]
-    expert_count = experts_local * dp_count
-    choose_count = expert_ids.shape[1]
-    capacity = max(2, 2 * share_rows * choose_count // expert_count)
-    flat = expert_ids.reshape(-1)
-    onehot = (flat[:, None] == jnp.arange(expert_count, dtype=jnp.int32)[None, :]).astype(jnp.int32)
-    earlier = jnp.cumsum(onehot, axis=0) - onehot
-    position = jnp.sum(earlier * onehot, axis=1)
-    target = flat * capacity + position
-    places = jnp.arange(expert_count * capacity, dtype=jnp.int32)
-    dispatch_mat = (target[None, :] == places[:, None]).astype(jnp.bfloat16)
-    repeated = jnp.repeat(normed, choose_count, axis=0)
-    outgoing = jnp.dot(dispatch_mat, repeated, preferred_element_type=jnp.float32).astype(
-        jnp.bfloat16
-    )
-    outgoing = outgoing.reshape(dp_count, experts_local * capacity, width)
-    arrived_rows = lax.all_to_all(outgoing, "dp", split_axis=0, concat_axis=0, tiled=True)
-    shared = lax.all_gather(arrived_rows[None], "head", axis=0, tiled=True)
-    tokens = shared.reshape(head_count * dp_count, experts_local * capacity, width)
-    sources = tokens.shape[0]
-    inputs = tokens.reshape(sources, experts_local, capacity, width)
-    gate_val = jnp.einsum("secd,edf->secf", inputs, w_gate, preferred_element_type=jnp.float32)
-    up_val = jnp.einsum("secd,edf->secf", inputs, w_up, preferred_element_type=jnp.float32)
-    act = (jax.nn.silu(gate_val) * up_val).astype(jnp.bfloat16)
-    result = jnp.einsum("secf,efd->secd", act, w_down, preferred_element_type=jnp.float32)
-    result = result.reshape(sources, experts_local * capacity, width)
-    result = result.reshape(head_count, dp_count, experts_local * capacity, width)
-    summed_out = lax.psum_scatter(result, "head", scatter_dimension=0, tiled=True)
-    returned = lax.all_to_all(summed_out[0], "dp", split_axis=0, concat_axis=0, tiled=True)
-    returned = returned.reshape(expert_count * capacity, width)
-    combine = jnp.sum(
-        jnp.where(
-            target.reshape(share_rows, choose_count)[:, :, None] == places[None, None, :],
-            gates[:, :, None],
-            jnp.zeros((), jnp.float32),
-        ),
-        axis=1,
-    )
-    moe_sum = jnp.dot(
-        combine, returned, precision=lax.Precision.HIGHEST, preferred_element_type=jnp.float32
-    )
-    return (hidden_one + moe_sum).astype(jnp.bfloat16)
+    rows = gather_rows(normed)
+    partial_out = experts(rows, codes, w_gate, w_up, w_down)
+    return reduce_rows(partial_out, hidden_one)
 
 
 def solution(mesh):

time: 529 us -> 329 us (0.62)
  waiting for transfers between devices: 392 us -> 61.3 us
  Pallas kernels: 0 us -> 108 us
  matrix products: 42.8 us -> 63.6 us
  blocking collectives: 32.3 us -> 53 us
  local copies, waits for them, and re-layouts: 28 us -> 15.7 us
  starting transfers between devices: 14.6 us -> 4.09 us
    reduce_scatter x1 -> x0, waiting for transfers between devices: 149 us -> none  [on_device(): lax.psum_scatter(result, 'head', scatter_dimension=0, tiled=True)]
    pallas_call x0 -> x2, Pallas kernels: none -> 108 us  [the longest x1 55.4 us: gather_rows(): pl.pallas_call(gather_kernel, out_shape=jax.ShapeDtypeStruct((2, SIDE, SI...]
    all_gather x1 -> x0, waiting for transfers between devices: 80.4 us -> none  [on_device(): shared = lax.all_gather(arrived_rows[None], 'head', axis=0, tiled=True)]
    all_to_all x1 -> x0, waiting for transfers between devices: 53.1 us -> none  [on_device(): lax.all_to_all(summed_out[0], 'dp', split_axis=0, concat_axis=0, tiled=True)]
    all_gather x0 -> x1, blocking collectives: none -> 53 us  [on_device(): lax.all_gather(route_codes(expert_ids, route_weights), ('dp', 'head'), ax...]
    psum x1, waiting for transfers between devices: 45.5 us -> 0.01 us  [on_device(): summed_proj = lax.psum(ordered, 'head')]
    all_to_all x1 -> x0, blocking collectives: 32.3 us -> none  [on_device(): lax.all_to_all(outgoing, 'dp', split_axis=0, concat_axis=0, tiled=True)]
    dot_general x5 -> x4, matrix products: 26.7 us -> 47.5 us  [the longest x1 15.2 us: experts(): jnp.einsum('gesf,efd->gesd', act, w_down, preferred_element_type=jnp.floa...]
  transfers between devices with their start and end apart: 6 -> 3, of which waited for: 6 -> 2; matrix products, arithmetic and copies ran while one was open for 0% -> 1% of each run, Pallas kernels for 0% -> 0%
where the time goes in v1:
time: 329 us; the launch traced here: 328 us
  Pallas kernels  108 us (33%)
  matrix products  63.6 us (19%)
  waiting for transfers between devices  61.3 us (19%)
  blocking collectives  53 us (16%)
  local copies, waits for them, and re-layouts  15.7 us (5%)
  between operations  14.5 us (4%)
  other arithmetic  8.14 us (2%)
  starting transfers between devices  4.09 us (1%)
    pallas_call x1, Pallas kernels, gather_rows(): pl.pallas_call(gather_kernel, out_shape=jax.ShapeDtypeStruct((2, SIDE, SI...  55.4 us
    all_gather x1, waiting for transfers between devices, on_device(): lax.all_gather(attn, 'dp', axis=0, tiled=True)  54.2 us
    all_gather x1, blocking collectives, on_device(): lax.all_gather(route_codes(expert_ids, route_weights), ('dp', 'head'), ax...  53 us
    pallas_call x1, Pallas kernels, reduce_rows(): pl.pallas_call(reduce_kernel, out_shape=jax.ShapeDtypeStruct((BLOCK, WIDT...  52.5 us
    dot_general x1, matrix products, experts(): jnp.einsum('gesf,efd->gesd', act, w_down, preferred_element_type=jnp.floa...  15.2 us
    dot_general x1, matrix products, experts(): jnp.einsum('gsr,grd->gsd', pick, tokens, preferred_element_type=jnp.float32)  11.7 us
    dot_general x1, matrix products, experts(): jnp.einsum('gsr,gsd->grd', pick, result, preferred_element_type=jnp.float32)  11.5 us
    dot_general x1, matrix products, experts(): jnp.einsum('gesd,edf->gesf', chosen, w_gate, preferred_element_type=jnp.f...  9.19 us
  transfers between devices with their start and end apart: 3, of which 2 were waited for; matrix products, arithmetic and copies ran while one was open for 1% of the time, Pallas kernels for 0%

profile of v1, /device:TPU:0, one launch (start us, length us, event | category | flops | bytes accessed | tf_op | source)
XLA Modules:
  0.0 328.3 jit_solution(9192869415194845064)
XLA Ops:
  6.5 1.4 reduce_max.18
  8.7 0.7 iota_compare_fusion.2
  9.4 0.7 convert_element_type.56
  10.2 1.0 copy.84
  11.3 5.6 %while.20 = (s32[]{:T(128)}, f32[64,1,16,256]{3,2,0,1:T(8,128)S(1)}, s32[]{:T(128)}, bf16[64,1,256,128]{3,2,0,1:T(8,128)(2,1)}, bf16[64,1,16,128]{3,2,0,1:T(8,12...) while((s32[]{:T(128)}, f32[64,1,16,256]{3,2,0,1:T(8,128)S(1)}, s32[]{:T(128)}, ...), condition=%wide.region_7.8_spmd, body=%wide.region_6.7_spmd.sunk | while | flops 33685508 | bytes 2884747 | solution.py:340
  11.3 2.8 fusion.74
  14.1 2.8 fusion.74
  17.4 0.5 fusion.43
  17.9 0.4 divide_convert_fusion
  18.4 4.5 %while.21 = (s32[]{:T(128)}, f32[64,1,16,128]{3,2,0,1:T(8,128)S(1)}, s32[]{:T(128)}, bf16[64,1,16,256]{3,2,0,1:T(8,128)(2,1)S(1)}, bf16[64,1,256,128]{3,2,0,1:T(...) while((s32[]{:T(128)}, f32[64,1,16,128]{3,2,0,1:T(8,128)S(1)}, s32[]{:T(128)}, ...), condition=%wide.region_11.12_spmd, body=%wide.region_10.11_spmd.sunk | while | flops 33685508 | bytes 3409035 | solution.py:360
  18.4 2.3 fusion.77
  20.7 2.3 fusion.77
  23.1 0.8 copy.100
  25.2 54.2 %all-gather.4.cloned.1.call-done = bf16[2048,2048]{1,0:T(8,128)(2,1)} async-done(((bf16[64,2048]{1,0:T(8,128)(2,1)}), bf16[2048,2048]{1,0:T(8,128)(2,1)}) %all-gather.4.cloned.1.call-update) | async-done | bytes 8388624 | tf_op jit(solution)/shard_map/all_gather | solution.py:435
  79.3 5.8 %fusion.59 = f32[2048,128]{1,0:T(8,128)S(1)} fusion(bf16[2048,2048]{1,0:T(8,128)(2,1)} %all-gather.4.cloned.1.call-done, bf16[2048,128]{1,0:T(8,128)(2,1)S(1)} %copy-done), kind=kOutput, calls=%fused_computation.83 | convolution fusion | flops 1073741824 | bytes 9961472 | tf_op jit(solution)/shard_map/dot_general | solution.py:434
  85.1 1.1 copy.68
  86.3 53.0 %all-gather.1 = f32[128,2,128]{2,1,0:T(2,128)S(1)} all-gather(f32[1,2,128]{2,1,0:T(2,128)S(1)} %maximum_bitcast_fusion), channel_id=2, replica_groups=mesh['dp'=32,'head'=4] {'dp','head'}, dimensions={0}, use_global_device_ids=true | all-gather | bytes 132096 | tf_op jit(solution)/shard_map/all_gather | solution.py:428
  139.3 0.4 reshape.199
  139.9 0.8 select_reduce_fusion.2
  141.3 1.7 constant_dynamic-slice_fusion
  143.0 4.0 %all-to-all-start = ((f32[32,16,128]{2,1,0:T(8,128)}), f32[32,16,128]{2,1,0:T(8,128)S(1)}, u32[]{:S(2)}, u32[]{:S(2)}) async-start(f32[32,16,128]{2,1,0:T(8,128)} %bitcast.19), calls=%async_computation | async-start | bytes 524288 | tf_op jit(solution)/shard_map/all_to_all | solution.py:447
  147.4 1.2 add_reduce_fusion
  148.7 7.1 %all-to-all-done = f32[32,16,128]{2,1,0:T(8,128)S(1)} async-done(((f32[32,16,128]{2,1,0:T(8,128)}), f32[32,16,128]{2,1,0:T(8,128)S(1)}, u32[]{:S(2)}, u32[]{:S(2)}) %all-to-all-start) | async-done | bytes 262176 | tf_op jit(solution)/shard_map/all_to_all | solution.py:447
  156.0 0.7 multiply_convert_fusion.mine_ref
  156.8 55.4 %shard_map.136 = bf16[2,4,4,4,16,4096]{5,4,3,2,1,0:T(8,128)(2,1)} custom-call(bf16[16,4096]{1,0:T(8,128)(2,1)} %multiply_convert_fusion.mine_ref), custom_call_target="tpu_custom_call" | custom-call | tf_op jit(solution)/shard_map/pallas_call | solution.py:135
  212.2 11.7 %convolution_convert_fusion.1 = bf16[8,128,4096]{2,1,0:T(8,128)(2,1)} fusion(bf16[8,256,4096]{2,1,0:T(8,128)(2,1)} %bitcast.133, f32[8,256]{1,0:T(8,128)S(1)} %get-tuple-element.146, f32[8,256]{1,0:T(8,128)S(1)} %get-tuple-element.145), kind=kOutput, calls=%fused_computation.18 | convolution fusion | flops 2152464384 | bytes 25182208 | tf_op jit(solution)/shard_map/gsr,grd->gsd/dot_general | solution.py:398
  223.9 9.2 %fusion.28 = f32[2,8,64,384]{3,2,1,0:T(8,128)S(1)} fusion(bf16[8,2,64,4096]{3,2,1,0:T(8,128)(2,1)} %bitcast.138, bf16[2,4096,384]{2,1,0:T(8,128)(2,1)} %param.29), kind=kOutput, calls=%fused_computation.21 | convolution fusion | flops 3221225472 | bytes 16252928 | tf_op jit(solution)/shard_map/gesd,edf->gesf/dot_general | solution.py:401
  233.1 15.2 %convert_bitcast_fusion = bf16[8,2,64,4096]{3,2,0,1:T(8,128)(2,1)} fusion(bf16[2,384,4096]{2,1,0:T(8,128)(2,1)} %param.31, f32[2,8,64,384]{3,2,1,0:T(8,128)S(1)} %fusion.28, bf16[2,4096,384]{2,1,0:T(8,128)(2,1)} %param.30, bf16[8,2,64,4096]{3,2,1,0:T(8,128)(2,1)} %bitcast.139, f32[8,2,64]{2,0,1:T(8,128)S(1)} %copy.75), kind=kOutput, calls=%fused_computation.17 | convolution fusion | flops 6449397760 | bytes 30937088 | tf_op jit(solution)/shard_map/gesf,efd->gesd/dot_general | solution.py:404
  248.2 7.7 %copy.76 = bf16[8,2,64,4096]{3,2,1,0:T(8,128)(2,1)} copy(bf16[8,2,64,4096]{3,2,0,1:T(8,128)(2,1)} %convert_bitcast_fusion) | data formatting | bytes 16777216 | tf_op jit(solution)/shard_map/convert_element_type | solution.py:404
  255.9 11.5 %convolution_convert_fusion = bf16[8,256,4096]{2,1,0:T(8,128)(2,1)} fusion(bf16[8,128,4096]{2,1,0:T(8,128)(2,1)} %bitcast.135, f32[8,256]{1,0:T(8,128)S(1)} %get-tuple-element.146, f32[8,256]{1,0:T(8,128)S(1)} %get-tuple-element.145), kind=kOutput, calls=%fused_computation.16 | convolution fusion | flops 2156658688 | bytes 25182208 | tf_op jit(solution)/shard_map/gsr,gsd->grd/dot_general | solution.py:406
  267.4 52.5 %shard_map.137 = bf16[16,4096]{1,0:T(8,128)(2,1)} custom-call(bf16[2,4,4,4,16,4096]{5,4,3,2,1,0:T(8,128)(2,1)} %bitcast.134, f32[16,4096]{1,0:T(8,128)} %copy-done.2), custom_call_target="tpu_custom_call" | custom-call | tf_op jit(solution)/shard_map/pallas_call | solution.py:289
  319.9 1.6 copy.116
  (62 shorter events, 3.5 us)
Async XLA Ops:
  6.5 72.8 %copy-start = (bf16[2048,128]{1,0:T(8,128)(2,1)S(1)}, bf16[2048,128]{1,0:T(8,128)(2,1)}, u32[]{:S(2)}) copy-start(bf16[2048,128]{1,0:T(8,128)(2,1)} %param.24) | copy-start | bytes 1572868
  6.5 72.8 %all-gather.4.cloned.1.call-start = ((), (), s32[]{:S(2)}) async-start(), calls=%async_computation.1 | async-start | bytes 8650752 | tf_op jit(solution)/shard_map/all_gather | solution.py:435
  11.3 5.6 %copy-start.7 = (bf16[64,128]{1,0:T(8,128)(2,1)S(1)}, bf16[64,128]{1,0:T(8,128)(2,1)}, u32[]{:S(2)}) copy-start(bf16[64,128]{1,0:T(8,128)(2,1)} %param.19) | copy-start | bytes 49156
  18.3 5.7 %copy-start.6 = (f32[16,8]{0,1:T(8,128)S(1)}, f32[16,8]{0,1:T(8,128)}, u32[]{:S(2)}) copy-start(f32[16,8]{0,1:T(8,128)} %param.28) | copy-start | bytes 1540
  18.3 5.9 %copy-start.5 = (s32[16,8]{0,1:T(8,128)S(1)}, s32[16,8]{0,1:T(8,128)}, u32[]{:S(2)}) copy-start(s32[16,8]{0,1:T(8,128)} %param.27) | copy-start | bytes 1540
  23.9 117.4 %all-reduce.2.cloned.1.call-start = ((), (), s32[]{:S(2)}) async-start(), calls=%async_computation.2 | async-start | bytes 2097152 | tf_op jit(solution)/shard_map/psum | solution.py:443
  85.1 70.7 %copy-start.3 = (bf16[16,4096]{1,0:T(8,128)(2,1)S(1)}, bf16[16,4096]{1,0:T(8,128)(2,1)}, u32[]{:S(2)}) copy-start(bf16[16,4096]{1,0:T(8,128)(2,1)} %param.25) | copy-start | bytes 393220
  85.1 70.9 %copy-start.4 = (f32[4096]{0:T(1024)S(1)}, f32[4096]{0:T(1024)}, u32[]{:S(2)}) copy-start(f32[4096]{0:T(1024)} %param.26) | copy-start | bytes 49156
  143.0 12.8 %all-to-all-start = ((f32[32,16,128]{2,1,0:T(8,128)}), f32[32,16,128]{2,1,0:T(8,128)S(1)}, u32[]{:S(2)}, u32[]{:S(2)}) async-start(f32[32,16,128]{2,1,0:T(8,128)} %bitcast.19), calls=%async_computation | async-start | bytes 524288 | tf_op jit(solution)/shard_map/all_to_all | solution.py:447
  156.0 56.2 %copy-start.2 = (f32[16,4096]{1,0:T(8,128)}, f32[16,4096]{1,0:T(8,128)S(1)}, u32[]{:S(2)}) copy-start(f32[16,4096]{1,0:T(8,128)S(1)} %get-tuple-element.140.base_ref) | copy-start | bytes 786436
  267.4 54.1 %copy-start.1 = (bf16[2048,128]{1,0:T(8,128)(2,1)S(1)}, bf16[2048,128]{1,0:T(8,128)(2,1)}, u32[]{:S(2)}) copy-start(bf16[2048,128]{1,0:T(8,128)(2,1)} %param.24) | copy-start | bytes 1572868
Sparse Core Ops, SparseCore 0:
  24.1 55.2 all-gather.3
  86.4 45.6 all-reduce.1

commit v2 on v0

v2 whole, which is shorter than its diff:
```python
import math

import jax
import jax.numpy as jnp
from jax import lax
from jax.experimental import pallas as pl
from jax.experimental.pallas import tpu as pltpu
from jax.sharding import PartitionSpec as P

MESH = pl.DeviceIdType.MESH
SIDE = 4
WIDTH = 4096
BLOCK = 16
CAPACITY = 4
CHOICES = 8
SLOTS = 64
ORDERS = (("x", "y", "z"), ("y", "z", "x"), ("z", "x", "y"))
WAVES = 2
PARTS = ORDERS * WAVES
WIDE = WIDTH + 256
TILES_OUT = (6, 6, 5)
TILES_BACK = (6, 6, 6, 5, 5, 4)
DIRECT_OUT = ((0, 0), (0, 1))
DIRECT_BACK = ((1, 1), (1, 2))
WIDEST = 768


def columns_of(tiles, part):
    return 128 * sum(tiles[:part]), 128 * tiles[part]


def my_place():
    row = lax.axis_index("dp")
    return {
        "y": row // (2 * SIDE),
        "x": (row // 2) % SIDE,
        "c": row % 2,
        "z": lax.axis_index("head"),
    }


def device_of(place):
    return ((place["y"] * SIDE + place["x"]) * 2 + place["c"], place["z"])


def shifted(place, axis, by):
    other = dict(place)
    other[axis] = (place[axis] + by) % SIDE
    return other


def sibling_of(place):
    other = dict(place)
    other["c"] = 1 - place["c"]
    return other


def greet(partners):
    barrier = pltpu.get_barrier_semaphore()
    for partner in partners:
        pl.semaphore_signal(barrier, inc=1, device_id=device_of(partner), device_id_type=MESH)
    pl.semaphore_wait(barrier, len(partners))


def remote(src, dst, send, recv, place):
    return pltpu.make_async_remote_copy(
        src_ref=src, dst_ref=dst, send_sem=send, recv_sem=recv,
        device_id=device_of(place), device_id_type=MESH,
    )


def blocks_at(ref, core, place, free, halves, columns):
    index = [core]
    last = max(free, key="zyx".index, default=None)
    for axis in ("z", "y", "x"):
        if axis in free:
            if halves is not None and axis == last:
                index.append(pl.ds(halves * (SIDE // 2), SIDE // 2))
            else:
                index.append(slice(None))
        else:
            index.append(place[axis])
    start, size = columns
    if not free and halves is not None:
        low = (size // 256) * 128
        start, size = (start, low) if halves == 0 else (start + low, size - low)
    return ref.at[(*index, slice(None), pl.ds(start, size))]


def attend_rows(base, rows, lengths_ref, query_ref, fresh_key_ref, fresh_value_ref, keys, values, attn_ref):
    slots, head_size = keys.shape[1:]
    heads = query_ref.shape[1] // head_size
    factor = 1.0 / math.sqrt(head_size)
    slot = lax.broadcasted_iota(jnp.int32, (heads, slots), 1)
    block = pl.ds(base, rows)
    query = jnp.stack([query_ref[block, head * head_size : (head + 1) * head_size].astype(jnp.float32) for head in range(heads)])
    query = jnp.swapaxes(query, 0, 1)
    narrow = query.astype(jnp.bfloat16)
    scores = []
    for row in range(rows):
        score = lax.dot_general(narrow[row], keys[base + row], (((1,), (1,)), ((), ())), preferred_element_type=jnp.float32)
        scores.append(jnp.where(slot < lengths_ref[base + row], score * factor, -1e30))
    scores = jnp.concatenate(scores, axis=0)
    fresh_key = fresh_key_ref[block].astype(jnp.float32).reshape(rows, 1, head_size)
    fresh = jnp.sum(query * fresh_key, axis=-1, keepdims=True).reshape(rows * heads, 1) * factor
    highest = jnp.maximum(jnp.max(scores, axis=-1, keepdims=True), fresh)
    spread = jnp.exp(scores - highest)
    fresh_exp = jnp.exp(fresh - highest)
    inverse = 1.0 / (jnp.sum(spread, axis=-1, keepdims=True) + fresh_exp)
    weights = (spread * inverse).astype(jnp.bfloat16)
    fresh_weight = (fresh_exp * inverse).astype(jnp.bfloat16).astype(jnp.float32)
    mixed = [
        jnp.dot(weights[row * heads : (row + 1) * heads], values[base + row], preferred_element_type=jnp.float32)
        for row in range(rows)
    ]
    fresh_value = fresh_value_ref[block].astype(jnp.float32).reshape(rows, 1, head_size)
    mixed = jnp.concatenate(mixed, axis=0).reshape(rows, heads, head_size) + fresh_weight.reshape(rows, heads, 1) * fresh_value
    mixed = jnp.swapaxes(mixed, 0, 1).astype(jnp.bfloat16)
    for head in range(heads):
        attn_ref[block, head * head_size : (head + 1) * head_size] = mixed[head]


def route_block(names_ref, names, weights, table):
    choices, rows = names.shape
    lane = lax.broadcasted_iota(jnp.int32, (choices, rows), 1)
    position = jnp.zeros((choices, rows), jnp.int32)
    for row in range(rows):
        same = names == names_ref[0, row]
        for choice in range(1, choices):
            same = same | (names == names_ref[choice, row])
        position += jnp.where(same & (lane > row), 1, 0)
    gates = weights / jnp.sum(weights, axis=0, keepdims=True)
    upper = gates.astype(jnp.bfloat16).astype(jnp.float32)
    table[...] = jnp.zeros_like(table)
    table[0:choices, 0:rows] = (names * CAPACITY + position).astype(jnp.float32)
    table[choices : 2 * choices, 0:rows] = upper
    table[2 * choices : 3 * choices, 0:rows] = gates - upper
    return table[...].T[0:rows].astype(jnp.bfloat16)


def attend_and_project_kernel(lengths_ref, names_ref, query_in, fresh_key_in, fresh_value_in, key_ref, value_ref,
                              weight_ref, residual_in, gain_in, names_in, weights_in, hidden_ref, normed_ref,
                              query_ref, fresh_key_ref, fresh_value_ref, residual_ref, gain_ref, names_here, weights_here, table,
                              attn_ref, keys, values, attn_all, weight_all, sums, sums_in, mine, mine_in,
                   local_sem, input_sem, key_sem, value_sem, w_send, w_recv, a_send, a_recv, p_send, p_recv, s_send, s_recv, m_send, m_recv):
    me = my_place()
    sibling = sibling_of(me)
    rows, depth = attn_ref.shape
    inputs = [
        pltpu.make_async_copy(src, dst, input_sem.at[at])
        for at, (src, dst) in enumerate((
            (query_in, query_ref), (fresh_key_in, fresh_key_ref), (fresh_value_in, fresh_value_ref), (residual_in, residual_ref),
            (gain_in, gain_ref), (names_in, names_here), (weights_in, weights_here),
        ))
    ]
    for load in inputs:
        load.start()
    own_cols = weight_ref.shape[1]
    half_depth, half_rows = depth // 2, rows // 2
    step = 16
    loads = []
    for at in range(rows // step):
        block = pl.ds(at * step, step)
        loads.append((pltpu.make_async_copy(key_ref.at[block, 0], keys.at[block], key_sem.at[at]),
                      pltpu.make_async_copy(value_ref.at[block, 0], values.at[block], value_sem.at[at])))
        for load in loads[-1]:
            load.start()

    def neighbour(by, core):
        other = shifted(me, "x", by)
        other["c"] = (me["c"] + core) % 2
        return other

    others = [(by, core) for by in range(SIDE) for core in range(2) if by or core]
    greet([neighbour(*which) for which in others] + [shifted(me, axis, by) for axis in "yz" for by in (1, 2, 3)])

    def weight_at(by, low=0, size=depth):
        column = ((me["y"] + by) % SIDE) * own_cols
        return weight_all.at[pl.ds(low, size), pl.ds(pl.multiple_of(column, own_cols), own_cols)]

    def attn_at(by, core, low=0, size=rows):
        return attn_all.at[(me["x"] + by) % SIDE, core, pl.ds(low, size)]

    core = me["c"]
    own_w = pltpu.make_async_copy(weight_ref, weight_at(0), local_sem.at[0])
    own_w.start()
    started = []

    def go(src, dst, send, recv, place):
        copy = remote(src, dst, send, recv, place)
        copy.start()
        started.append(copy)
        return copy

    near_w, near_a, far_w, far_a, pair = {}, {}, {}, {}, {}
    for way, by in ((0, 1), (1, -1)):
        near_w[way] = go(weight_ref, weight_at(0), w_send.at[way], w_recv.at[way], shifted(me, "y", by))
    for load in inputs:
        load.wait()
    for at in range(rows // step):
        for load in loads[at]:
            load.wait()
        attend_rows(at * step, step, lengths_ref, query_ref, fresh_key_ref, fresh_value_ref, keys, values, attn_ref)
    own_a = pltpu.make_async_copy(attn_ref, attn_at(0, core), local_sem.at[1])
    own_a.start()
    for way, by in ((0, 1), (1, -1)):
        near_a[way] = go(attn_ref, attn_at(0, core), a_send.at[way], a_recv.at[way], shifted(me, "x", by))
    pair[0] = go(attn_ref, attn_at(0, core), p_send.at[0], p_recv.at[0], sibling)
    for way, by in ((0, 1), (1, -1)):
        near_w[way].wait_recv()
        block = weight_at(-by, way * half_depth, half_depth)
        far_w[way] = go(block, block, w_send.at[2 + way], w_recv.at[2 + way], shifted(me, "y", by))
    for way, by in ((0, 1), (1, -1)):
        near_a[way].wait_recv()
        block = attn_at(-by, core, way * half_rows, half_rows)
        far_a[way] = go(block, block, a_send.at[2 + way], a_recv.at[2 + way], shifted(me, "x", by))
        block = attn_at(-by, core)
        pair[-by] = go(block, block, p_send.at[1 + way], p_recv.at[1 + way], sibling)
    for way in (0, 1):
        far_a[way].wait_recv()
    block = attn_at(2, core)
    pair[2] = go(block, block, p_send.at[3], p_recv.at[3], sibling)
    normed_ref[:, WIDTH : WIDTH + 128] = route_block(names_ref, names_here[...], weights_here[...], table)
    normed_ref[:, WIDTH + 128 :] = jnp.zeros((rows // SIDE, WIDE - WIDTH - 128), normed_ref.dtype)
    own_w.wait()
    own_a.wait()
    for way in (0, 1):
        far_w[way].wait_recv()

    share = rows // SIDE
    width = weight_all.shape[1]
    order = (0, 1, -1, 2)
    to_head = {}
    for number, by in enumerate(order):
        pair[by].wait_recv()
        at = (me["x"] + by) % SIDE
        block = attn_all[at].reshape(2 * rows, depth)
        part = jnp.dot(block, weight_all[...], preferred_element_type=jnp.float32).astype(jnp.bfloat16)
        part = part.reshape(2, SIDE, share, width)
        for head in range(SIDE):
            sums[head, at] = part[:, head]
        for away in (1, 2, 3):
            target = shifted(me, "z", away)
            to_head[number, away] = go(sums.at[target["z"], at], sums_in.at[away - 1, at],
                                       s_send.at[number, away - 1], s_recv.at[number, away - 1], target)
    slots = {}
    for number, by in enumerate(order):
        at = (me["x"] + by) % SIDE
        for away in (1, 2, 3):
            to_head[number, away].wait_recv()
        total = sums[me["z"], at].astype(jnp.float32)
        for away in range(3):
            total += sums_in[away, at].astype(jnp.float32)
        mine[number] = total.astype(jnp.bfloat16)
        for flip in (0, 1):
            if by == 0 and flip == 0:
                continue
            target = neighbour(by, flip)
            slots[number, flip] = go(mine.at[number, target["c"]], mine_in.at[me["x"], core],
                                     m_send.at[number, flip], m_recv.at[number, flip], target)
    keep = pltpu.make_async_copy(mine.at[0, core], mine_in.at[me["x"], core], local_sem.at[2])
    keep.start()
    keep.wait()
    for copy in slots.values():
        copy.wait_recv()
    square = jnp.zeros((share, 1), jnp.float32)
    for y in range(SIDE):
        for x in range(SIDE):
            for c in range(2):
                start = ((y * SIDE + x) * 2 + c) * own_cols
                value = residual_ref[:, start : start + own_cols].astype(jnp.float32)
                value += mine_in[x, c, :, y * own_cols : (y + 1) * own_cols].astype(jnp.float32)
                hidden_ref[:, start : start + own_cols] = value
                square += jnp.sum(value * value, axis=-1, keepdims=True)
    scale = lax.rsqrt(square / WIDTH + 1e-06)
    for start in range(0, WIDTH, 512):
        normed_ref[:, start : start + 512] = (hidden_ref[:, start : start + 512] * scale * gain_ref[:, start : start + 512]).astype(jnp.bfloat16)
    for copy in started:
        copy.wait_send()


def attend_and_project(queries, new_keys, new_values, key_cache, value_cache, cache_lengths, out_weight, residual, gain, expert_ids, route_weights):
    rows, _, slots, head_size = key_cache.shape
    depth = queries.shape[1]
    own_cols = out_weight.shape[1]
    width = SIDE * own_cols
    share = rows // SIDE
    vmem, hbm, smem = (pl.BlockSpec(memory_space=space) for space in (pltpu.VMEM, pl.ANY, pltpu.SMEM))
    names, route_weights = expert_ids.T, route_weights.T
    bf16 = jnp.bfloat16
    dma = pltpu.SemaphoreType.DMA
    return pl.pallas_call(
        attend_and_project_kernel,
        out_shape=(
            jax.ShapeDtypeStruct((share, WIDTH), jnp.float32),
            jax.ShapeDtypeStruct((share, WIDE), bf16),
        ),
        in_specs=[smem, smem] + [hbm] * 10,
        out_specs=(vmem, vmem),
        scratch_shapes=[
            pltpu.VMEM((rows, depth), bf16),
            pltpu.VMEM(new_keys.shape, bf16),
            pltpu.VMEM(new_values.shape, bf16),
            pltpu.VMEM(residual.shape, bf16),
            pltpu.VMEM((1, WIDTH), jnp.float32),
            pltpu.VMEM(names.shape, jnp.int32),
            pltpu.VMEM(names.shape, jnp.float32),
            pltpu.VMEM((128, 128), jnp.float32),
            pltpu.VMEM((rows, depth), bf16),
            pltpu.VMEM((rows, slots, head_size), bf16),
            pltpu.VMEM((rows, slots, head_size), bf16),
            pltpu.VMEM((SIDE, 2, rows, depth), bf16),
            pltpu.VMEM((depth, width), bf16),
            pltpu.VMEM((SIDE, SIDE, 2, share, width), bf16),
            pltpu.VMEM((SIDE - 1, SIDE, 2, share, width), bf16),
            pltpu.VMEM((SIDE, 2, share, width), bf16),
            pltpu.VMEM((SIDE, 2, share, width), bf16),
            dma((3,)), dma((7,)), dma((rows // 16,)), dma((rows // 16,)),
            dma((4,)), dma((4,)), dma((4,)), dma((4,)), dma((4,)), dma((4,)),
            dma((4, 3)), dma((4, 3)), dma((4, 2)), dma((4, 2)),
        ],
        compiler_params=pltpu.CompilerParams(collective_id=3, has_side_effects=True, vmem_limit_bytes=60 * 1024 * 1024),
    )(cache_lengths, names, queries, new_keys, new_values, key_cache, value_cache, out_weight, residual, gain.reshape(1, WIDTH), names, route_weights)


def pick_group(table):
    span = table.shape[0]
    lane = lax.broadcasted_iota(jnp.int32, table.shape, 1)
    row = lax.broadcasted_iota(jnp.int32, (span, 1), 0)
    place = (row // BLOCK * CAPACITY).astype(jnp.float32)
    first = (lax.axis_index("dp") * 2 * CAPACITY).astype(jnp.float32)
    spot = lane.astype(jnp.float32)
    picked = jnp.zeros(table.shape, jnp.float32)
    gates = jnp.zeros(table.shape, jnp.float32)
    for own in range(2):
        code = table - (first + own * CAPACITY)
        hit = jnp.where((lane < CHOICES) & (code >= 0) & (code < CAPACITY), 1.0, 0.0)
        slot = jnp.sum(hit * (code + 1), axis=-1, keepdims=True)
        slot = jnp.where(slot > 0, slot - 1 + place + own * SLOTS, -1.0)
        gate = jnp.sum(table * (pltpu.roll(hit, CHOICES, 1) + pltpu.roll(hit, 2 * CHOICES, 1)), axis=-1, keepdims=True)
        match = spot == slot
        picked += jnp.where(match, 1.0, 0.0)
        gates += jnp.where(match, gate, 0.0)
    scale = jnp.broadcast_to(jnp.sum(gates, axis=0, keepdims=True), (128, 128)).T
    return picked, scale


def open_kernel(mine_ref, gate_ref, up_ref, act_ref, pick_ref, everyone, gate_w, up_w, chosen, scales, gate_sum, up_sum,
                own_sem, weight_sem, near_send, near_recv, far_send, far_recv, pair_send, pair_recv, first_send, first_recv):
    me = my_place()
    core = me["c"]
    sibling = sibling_of(me)
    loads = [pltpu.make_async_copy(gate_ref, gate_w, weight_sem.at[0]), pltpu.make_async_copy(up_ref, up_w, weight_sem.at[1])]
    greet([sibling] + [shifted(me, axis, by) for axis in "xyz" for by in (1, 2, 3)])
    home = everyone.at[core, me["z"], me["y"], me["x"]]
    own = pltpu.make_async_copy(mine_ref, home, own_sem)
    own.start()
    first = remote(mine_ref, home, first_send, first_recv, sibling)
    first.start()
    own.wait()
    first.wait_recv()
    near, far, pair = {}, {}, {}

    def group(part, stage, coordinate_shift, halves=None):
        order = PARTS[part]
        place = shifted(me, order[stage], coordinate_shift)
        start, size = columns_of(TILES_OUT, part % 3)
        start = pl.multiple_of(core * (WIDE // 2) + start, 128)
        return blocks_at(everyone, part // 3, place, order[:stage], halves, (start, size))

    def to_pair(part, stage, number, block):
        copy = remote(block, block, pair_send.at[part, stage, number], pair_recv.at[part, stage, number], sibling)
        copy.start()
        pair[part, stage, number] = copy

    def send_near(wave, stage):
        for part in range(3 * wave, 3 * wave + 3):
            block = group(part, stage, 0)
            if (wave, stage) in DIRECT_OUT:
                copy = remote(block, block, far_send.at[part, stage, 0], far_recv.at[part, stage, 0], shifted(me, PARTS[part][stage], 2))
                copy.start()
                far[part, stage, 0] = copy
            for way, by in ((0, 1), (1, -1)):
                copy = remote(block, block, near_send.at[part, stage, way], near_recv.at[part, stage, way], shifted(me, PARTS[part][stage], by))
                copy.start()
                near[part, stage, way] = copy

    def send_far(wave, stage):
        for part in range(3 * wave, 3 * wave + 3):
            for way, by in ((0, 1), (1, -1)):
                near[part, stage, way].wait_recv()
                if (wave, stage) not in DIRECT_OUT:
                    block = group(part, stage, -by, way)
                    copy = remote(block, block, far_send.at[part, stage, way], far_recv.at[part, stage, way], shifted(me, PARTS[part][stage], by))
                    copy.start()
                    far[part, stage, way] = copy
                to_pair(part, stage, way, group(part, stage, -by))

    def take_far(wave, stage):
        for part in range(3 * wave, 3 * wave + 3):
            for way in (0, 1):
                if (part, stage, way) in far:
                    far[part, stage, way].wait_recv()
            to_pair(part, stage, 2, group(part, stage, 2))

    groups, span = pick_ref.shape[0], pick_ref.shape[1]

    def choose(at, _):
        c, z = at // SIDE, at % SIDE
        picked, scale = pick_group(everyone[c, z, :, :, :, WIDTH : WIDTH + 128].reshape(span, 128).astype(jnp.float32))
        pick_ref[at] = picked.astype(jnp.bfloat16)
        turned = picked.T.astype(jnp.bfloat16)
        for half in range(2):
            scales[half, at] = scale[half * SLOTS : half * SLOTS + SLOTS]
        for start in range(0, WIDTH, 512):
            rows = everyone[c, z, :, :, :, start : start + 512].reshape(span, 512)
            part = jnp.dot(turned, rows, preferred_element_type=jnp.float32).astype(jnp.bfloat16)
            for half in range(2):
                chosen[half, at, :, start : start + 512] = part[half * SLOTS : half * SLOTS + SLOTS]
        return 0

    depth = 1024
    share = groups // 2

    def open_one(wave, own):
        gate_sum[...] = jnp.zeros_like(gate_sum)
        up_sum[...] = jnp.zeros_like(up_sum)

        def multiply(step, _):
            columns = pl.ds(pl.multiple_of(step * depth, depth), depth)
            rows = chosen[own, wave * share : (wave + 1) * share, :, columns].reshape(share * SLOTS, depth)
            gate_sum[...] += jnp.dot(rows, gate_w[own, columns, :], preferred_element_type=jnp.float32)
            up_sum[...] += jnp.dot(rows, up_w[own, columns, :], preferred_element_type=jnp.float32)
            return 0

        lax.fori_loop(0, WIDTH // depth, multiply, 0)

        def finish(at, _):
            rows = pl.ds(pl.multiple_of(at * SLOTS, SLOTS), SLOTS)
            value = gate_sum[rows]
            there = pl.ds(pl.multiple_of((wave * share + at) * SLOTS, SLOTS), SLOTS)
            act_ref[own, there] = (value / (1.0 + jnp.exp(-value)) * up_sum[rows] * scales[own, wave * share + at][:, :1]).astype(jnp.bfloat16)
            return 0

        lax.fori_loop(0, share, finish, 0)

    def settle(wave):
        for (part, _, _), copy in pair.items():
            if part // 3 == wave:
                copy.wait_recv()
        lax.fori_loop(wave * share, (wave + 1) * share, choose, 0)

    send_near(0, 0)
    send_near(1, 0)
    for load in loads:
        load.start()
    send_far(0, 0)
    take_far(0, 0)
    send_near(0, 1)
    send_far(1, 0)
    take_far(1, 0)
    send_near(1, 1)
    send_far(0, 1)
    take_far(0, 1)
    send_near(0, 2)
    send_far(1, 1)
    take_far(1, 1)
    send_near(1, 2)
    send_far(0, 2)
    take_far(0, 2)
    settle(0)
    send_far(1, 2)
    for load in loads:
        load.wait()
    open_one(0, 0)
    open_one(0, 1)
    take_far(1, 2)
    settle(1)
    open_one(1, 0)
    open_one(1, 1)
    for copy in [first, *near.values(), *far.values(), *pair.values()]:
        copy.wait_send()


def gather_and_open(mine, w_gate, w_up):
    bf16, f32, dma = jnp.bfloat16, jnp.float32, pltpu.SemaphoreType.DMA
    groups, span = 2 * SIDE, SIDE * SIDE * BLOCK
    hidden = w_gate.shape[2]
    vmem, hbm = pl.BlockSpec(memory_space=pltpu.VMEM), pl.BlockSpec(memory_space=pl.ANY)
    parts = len(PARTS)
    return pl.pallas_call(
        open_kernel,
        out_shape=(
            jax.ShapeDtypeStruct((2, groups * SLOTS, hidden), bf16),
            jax.ShapeDtypeStruct((groups, span, 128), bf16),
        ),
        in_specs=[vmem, hbm, hbm],
        out_specs=(vmem, vmem),
        scratch_shapes=[
            pltpu.VMEM((2, SIDE, SIDE, SIDE, *mine.shape), bf16),
            pltpu.VMEM(w_gate.shape, bf16),
            pltpu.VMEM(w_up.shape, bf16),
            pltpu.VMEM((2, groups, SLOTS, WIDTH), bf16),
            pltpu.VMEM((2, groups, SLOTS, 128), f32),
            pltpu.VMEM((groups // 2 * SLOTS, hidden), f32),
            pltpu.VMEM((groups // 2 * SLOTS, hidden), f32),
            dma, dma((2,)),
            dma((parts, 3, 2)), dma((parts, 3, 2)), dma((parts, 3, 2)), dma((parts, 3, 2)),
            dma((parts, 3, 3)), dma((parts, 3, 3)), dma, dma,
        ],
        compiler_params=pltpu.CompilerParams(collective_id=1, has_side_effects=True, vmem_limit_bytes=60 * 1024 * 1024),
    )(mine, w_gate, w_up)

def close_kernel(act_ref, pick_ref, down_ref, out_ref, acc, pair_buf, down_w, result,
                 near0, near1, near2, far0, far1, far2,
                 weight_sem, pair_send, pair_recv, near_send, near_recv, far_send, far_recv):
    me = my_place()
    core = me["c"]
    sibling = sibling_of(me)
    near_bufs, far_bufs = (near0, near1, near2), (far0, far1, far2)
    loads = []
    for part in range(len(PARTS)):
        start, size = columns_of(TILES_BACK, part)
        columns = (slice(None), slice(None), pl.ds(start, size))
        loads.append(pltpu.make_async_copy(down_ref.at[columns], down_w.at[columns], weight_sem.at[part]))
        loads[-1].start()
    greet([sibling] + [shifted(me, axis, by) for axis in "xyz" for by in (1, 2, 3)])
    pair, near, far = {}, {}, {}
    groups, span = pick_ref.shape[0], pick_ref.shape[1]

    def axis_of(part, stage):
        return PARTS[part][2 - stage]

    def group(ref, part, stage, shift, which, halves=None):
        place = shifted(me, axis_of(part, stage), shift)
        return blocks_at(ref, which, place, PARTS[part][: 2 - stage], halves, columns_of(TILES_BACK, part))

    def multiply(part):
        loads[part].wait()
        start, size = columns_of(TILES_BACK, part)
        for own in range(2):
            product = jnp.dot(act_ref[own], down_w[own, :, start : start + size], preferred_element_type=jnp.float32)
            result[:, own, :, :size] = product.astype(jnp.bfloat16).reshape(groups, SLOTS, size)

        def spread(at, _):
            both = result[at, :, :, :size].reshape(2 * SLOTS, size)
            rows = jnp.dot(pick_ref[at], both, preferred_element_type=jnp.float32).astype(jnp.bfloat16)
            acc[at // SIDE, at % SIDE, :, :, :, start : start + size] = rows.reshape(SIDE, SIDE, BLOCK, size)
            return 0

        lax.fori_loop(0, groups, spread, 0)
        for number, shift in enumerate((2, 1, -1, 0)):
            copy = remote(
                group(acc, part, 0, shift, 1 - core), group(pair_buf, part, 0, shift, 0),
                pair_send.at[part, number], pair_recv.at[part, number], sibling,
            )
            copy.start()
            pair[part, number] = copy

    def add_into(target, others):
        lead = target.shape[:-2]
        count = math.prod(lead)

        def body(at, _):
            index = []
            rest = at
            for size in reversed(lead):
                index.insert(0, rest % size)
                rest = rest // size
            index = (*index, slice(None), slice(None))
            total = target[index].astype(jnp.float32)
            for other in others:
                total += other[index].astype(jnp.float32)
            target[index] = total.astype(target.dtype)
            return 0

        if count == 1:
            body(0, 0)
        else:
            lax.fori_loop(0, count, body, 0)

    def add_pair(part, number, shift):
        pair[part, number].wait_recv()
        add_into(group(acc, part, 0, shift, core), [group(pair_buf, part, 0, shift, 0)])

    def near_copy(part, stage, way, half):
        by = 1 if way == 0 else -1
        src = group(acc, part, stage, by, core, half)
        dst = near_bufs[stage].at[part, way, half, ..., pl.ds(0, src.shape[-1])]
        copy = remote(src, dst, near_send.at[part, stage, way, half], near_recv.at[part, stage, way, half], shifted(me, axis_of(part, stage), by))
        copy.start()
        near[part, stage, way, half] = copy

    def send_far(wave, stage):
        for part in range(3 * wave, 3 * wave + 3):
            if stage == 0:
                add_pair(part, 0, 2)
            for way, by in ((0, 1), (1, -1)):
                src = group(acc, part, stage, 2, core, way)
                dst = far_bufs[stage].at[part, way, ..., pl.ds(0, src.shape[-1])]
                by = 2 if (wave, stage) in DIRECT_BACK else by
                copy = remote(src, dst, far_send.at[part, stage, way], far_recv.at[part, stage, way], shifted(me, axis_of(part, stage), by))
                copy.start()
                far[part, stage, way] = copy

    def send_near(wave, stage):
        for part in range(3 * wave, 3 * wave + 3):
            for way, by in ((0, 1), (1, -1)):
                if stage == 0:
                    add_pair(part, 1 + way, by)
                near_copy(part, stage, way, 1 - way)
                if (wave, stage) in DIRECT_BACK:
                    near_copy(part, stage, way, way)

    def relay(wave, stage):
        if (wave, stage) in DIRECT_BACK:
            return
        for part in range(3 * wave, 3 * wave + 3):
            for way, by in ((0, 1), (1, -1)):
                far[part, stage, way].wait_recv()
                target = group(acc, part, stage, by, core, way)
                add_into(target, [far_bufs[stage].at[part, way, ..., pl.ds(0, target.shape[-1])]])
                near_copy(part, stage, way, way)

    def take(wave, stage):
        for part in range(3 * wave, 3 * wave + 3):
            if stage == 0:
                add_pair(part, 3, 0)
            for half in (0, 1):
                for way in (0, 1):
                    near[part, stage, way, half].wait_recv()
                target = group(acc, part, stage, 0, core, half)
                others = [near_bufs[stage].at[part, way, half, ..., pl.ds(0, target.shape[-1])] for way in (0, 1)]
                if (wave, stage) in DIRECT_BACK:
                    far[part, stage, half].wait_recv()
                    others.append(far_bufs[stage].at[part, half, ..., pl.ds(0, target.shape[-1])])
                if stage < 2:
                    add_into(target, others)
                else:
                    total = target[...].astype(jnp.float32)
                    for other in others:
                        total += other[...].astype(jnp.float32)
                    start, size = columns_of(TILES_BACK, part)
                    low = (size // 256) * 128
                    start, size = (start, low) if half == 0 else (start + low, size - low)
                    out_ref[:, pl.ds(start, size)] = total

    for part in range(3):
        multiply(part)
    send_far(0, 0)
    send_near(0, 0)
    for part in range(3, 6):
        multiply(part)
    relay(0, 0)
    send_far(1, 0)
    send_near(1, 0)
    take(0, 0)
    send_far(0, 1)
    send_near(0, 1)
    relay(1, 0)
    relay(0, 1)
    take(0, 1)
    send_far(0, 2)
    send_near(0, 2)
    take(1, 0)
    send_far(1, 1)
    send_near(1, 1)
    relay(0, 2)
    relay(1, 1)
    take(0, 2)
    take(1, 1)
    send_far(1, 2)
    send_near(1, 2)
    relay(1, 2)
    take(1, 2)
    for copy in [*pair.values(), *near.values(), *far.values()]:
        copy.wait_send()


def close_and_reduce(act, pick, w_down):
    bf16, dma = jnp.bfloat16, pltpu.SemaphoreType.DMA
    groups = pick.shape[0]
    half = SIDE // 2
    parts = len(PARTS)
    last = WIDEST // 2
    vmem, hbm = pl.BlockSpec(memory_space=pltpu.VMEM), pl.BlockSpec(memory_space=pl.ANY)
    return pl.pallas_call(
        close_kernel,
        out_shape=jax.ShapeDtypeStruct((BLOCK, WIDTH), jnp.float32),
        in_specs=[vmem, vmem, hbm],
        out_specs=vmem,
        scratch_shapes=[
            pltpu.VMEM((2, SIDE, SIDE, SIDE, BLOCK, WIDTH), bf16),
            pltpu.VMEM((1, SIDE, SIDE, SIDE, BLOCK, WIDTH), bf16),
            pltpu.VMEM(w_down.shape, bf16),
            pltpu.VMEM((groups, 2, SLOTS, WIDEST), bf16),
            pltpu.VMEM((parts, 2, 2, SIDE, half, BLOCK, WIDEST), bf16),
            pltpu.VMEM((parts, 2, 2, half, BLOCK, WIDEST), bf16),
            pltpu.VMEM((parts, 2, 2, BLOCK, last), bf16),
            pltpu.VMEM((parts, 2, SIDE, half, BLOCK, WIDEST), bf16),
            pltpu.VMEM((parts, 2, half, BLOCK, WIDEST), bf16),
            pltpu.VMEM((parts, 2, BLOCK, last), bf16),
            dma((parts,)), dma((parts, 4)), dma((parts, 4)),
            dma((parts, 3, 2, 2)), dma((parts, 3, 2, 2)), dma((parts, 3, 2)), dma((parts, 3, 2)),
        ],
        compiler_params=pltpu.CompilerParams(collective_id=2, has_side_effects=True, vmem_limit_bytes=60 * 1024 * 1024),
    )(act, pick, w_down)


def on_device(
    queries,
    new_keys,
    new_values,
    key_cache,
    value_cache,
    cache_lengths,
    out_weight,
    residual_in,
    norm_gain,
    expert_ids,
    route_weights,
    w_gate,
    w_up,
    w_down,
):
    hidden_one, normed = attend_and_project(
        queries, new_keys, new_values, key_cache, value_cache, cache_lengths, out_weight, residual_in, norm_gain,
        expert_ids, route_weights,
    )
    act, pick = gather_and_open(normed, w_gate, w_up)
    return (hidden_one + close_and_reduce(act, pick, w_down)).astype(jnp.bfloat16)


def solution(mesh):
    in_specs = (
        P("dp", "head"),
        P("dp", "head"),
        P("dp", "head"),
        P("dp", "head", None, None),
        P("dp", "head", None, None),
        P("dp"),
        P("head", "dp"),
        P(("dp", "head"), None),
        P(),
        P(("dp", "head"), None),
        P(("dp", "head"), None),
        P("dp", None, "head"),
        P("dp", None, "head"),
        P("dp", "head", None),
    )
    out_specs = P(("dp", "head"), None)
    return jax.shard_map(
        on_device, mesh=mesh, in_specs=in_specs, out_specs=out_specs, check_vma=False
    )
```

time: 529 us -> 175 us (0.33)
  waiting for transfers between devices: 392 us -> 0 us
  Pallas kernels: 0 us -> 173 us
  matrix products: 42.8 us -> 0 us
  blocking collectives: 32.3 us -> 0 us
  local copies, waits for them, and re-layouts: 28 us -> 0.01 us
  starting transfers between devices: 14.6 us -> 0 us
  between operations: 14.1 us -> 0.04 us
    pallas_call x0 -> x3, Pallas kernels: none -> 173 us  [the longest x1 71 us: gather_and_open(): pl.pallas_call(open_kernel, out_shape=(jax.ShapeDtypeStruct((2, groups *...]
    reduce_scatter x1 -> x0, waiting for transfers between devices: 149 us -> none  [on_device(): lax.psum_scatter(result, 'head', scatter_dimension=0, tiled=True)]
    all_gather x2 -> x0, waiting for transfers between devices: 136 us -> none  [the longest x1 80.4 us: on_device(): shared = lax.all_gather(arrived_rows[None], 'head', axis=0, tiled=True)]
    all_to_all x2 -> x0, waiting for transfers between devices: 61.8 us -> none  [the longest x1 53.1 us: on_device(): lax.all_to_all(summed_out[0], 'dp', split_axis=0, concat_axis=0, tiled=True)]
    psum x1 -> x0, waiting for transfers between devices: 45.5 us -> none  [on_device(): summed_proj = lax.psum(ordered, 'head')]
    dot_general x11 -> x0, matrix products: 42.8 us -> none  [the longest x1 9.08 us: on_device(): jnp.einsum('secd,edf->secf', inputs, w_gate, preferred_element_type=jnp.f...]
    all_to_all x1 -> x0, blocking collectives: 32.3 us -> none  [on_device(): lax.all_to_all(outgoing, 'dp', split_axis=0, concat_axis=0, tiled=True)]
    all_to_all x2 -> x0, starting transfers between devices: 14.3 us -> none  [the longest x1 7.35 us: on_device(): lax.all_to_all(summed_out[0], 'dp', split_axis=0, concat_axis=0, tiled=True)]
  transfers between devices with their start and end apart: 6 -> 0, of which waited for: 6 -> 0; matrix products, arithmetic and copies ran while one was open for 0% -> 0% of each run, Pallas kernels for 0% -> 0%
where the time goes in v2:
time: 175 us
  Pallas kernels  173 us (99%)
    pallas_call x1, Pallas kernels, gather_and_open(): pl.pallas_call(open_kernel, out_shape=(jax.ShapeDtypeStruct((2, groups *...  71 us
    pallas_call x1, Pallas kernels, close_and_reduce(): pl.pallas_call(close_kernel, out_shape=jax.ShapeDtypeStruct((BLOCK, WIDTH...  61.6 us
    pallas_call x1, Pallas kernels, attend_and_project(): pl.pallas_call(attend_and_project_kernel, out_shape=(jax.ShapeDtypeStruct...  40.3 us

profile of v2, /device:TPU:0, one launch (start us, length us, event | category | flops | bytes accessed | tf_op | source)
XLA Modules:
  0.0 174.6 jit_solution(1510583373457294494)
XLA Ops:
  0.0 40.3 %shard_map.136 = (f32[16,4096]{1,0:T(8,128)}, bf16[16,4352]{1,0:T(8,128)(2,1)}) custom-call(s32[64]{0:T(128)} %lengths_ref.1, s32[8,16]{1,0:T(8,128)} %bitcast.3, bf16[64,2048]{1,0:T(8,128)(2,1)} %query_in.1, bf16[64,128]{1,0:T(8,128)(2,1)} %fresh_key_in.1, bf16[64,128]{1,0:T(8,128)(2,1)} %fresh_value_in.1, bf16[64,1,256,128]{3,2,1,0:T(8,128)(2,1)} %key_ref.1, ...), custom_call_target="tpu_custom_call" | custom-call | tf_op jit(solution)/shard_map/pallas_call | solution.py:292
  40.3 71.0 %shard_map.137 = (bf16[2,512,384]{2,1,0:T(8,128)(2,1)}, bf16[8,256,128]{2,1,0:T(8,128)(2,1)}) custom-call(bf16[16,4352]{1,0:T(8,128)(2,1)} %get-tuple-element.10.mine_ref, bf16[2,4096,384]{2,1,0:T(8,128)(2,1)} %gate_ref.1, bf16[2,4096,384]{2,1,0:T(8,128)(2,1)} %up_ref.1), custom_call_target="tpu_custom_call" | custom-call | tf_op jit(solution)/shard_map/pallas_call | solution.py:491
  111.3 0.0 copy-start
  111.3 61.6 %shard_map.138 = f32[16,4096]{1,0:T(8,128)} custom-call(bf16[2,512,384]{2,1,0:T(8,128)(2,1)} %get-tuple-element.11.act_ref, bf16[8,256,128]{2,1,0:T(8,128)(2,1)} %get-tuple-element.12.pick_ref, bf16[2,384,4096]{2,1,0:T(8,128)(2,1)} %down_ref.1), custom_call_target="tpu_custom_call" | custom-call | tf_op jit(solution)/shard_map/pallas_call | solution.py:687
  172.9 0.0 copy-done
  172.9 1.6 add_convert_fusion
Async XLA Ops:
  111.3 61.6 %copy-start = (f32[16,4096]{1,0:T(8,128)S(1)}, f32[16,4096]{1,0:T(8,128)}, u32[]{:S(2)}) copy-start(f32[16,4096]{1,0:T(8,128)} %get-tuple-element.9) | copy-start | bytes 786436

commit v3 on v2

--- a/solution.py
+++ b/solution.py
@@ -142,7 +142,7 @@
                               weight_ref, residual_in, gain_in, names_in, weights_in, hidden_ref, normed_ref,
                               query_ref, fresh_key_ref, fresh_value_ref, residual_ref, gain_ref, names_here, weights_here, table,
                               attn_ref, keys, values, attn_all, weight_all, sums, sums_in, mine, mine_in,
-                   local_sem, input_sem, key_sem, value_sem, w_send, w_recv, a_send, a_recv, p_send, p_recv, s_send, s_recv, m_send, m_recv):
+                   local_sem, input_sem, key_sem, value_sem, w_send, w_recv, a_send, a_recv, f_send, f_recv, p_send, p_recv, s_send, s_recv, m_send, m_recv):
     me = my_place()
     sibling = sibling_of(me)
     rows, depth = attn_ref.shape
@@ -197,29 +197,40 @@
         near_w[way] = go(weight_ref, weight_at(0), w_send.at[way], w_recv.at[way], shifted(me, "y", by))
     for load in inputs:
         load.wait()
-    for at in range(rows // step):
+    def send_attn(half):
+        src, dst = attn_ref.at[pl.ds(half * half_rows, half_rows)], attn_at(0, core, half * half_rows, half_rows)
+        for way, by in ((0, 1), (1, -1)):
+            near_a[way, half] = go(src, dst, a_send.at[way, half], a_recv.at[way, half], shifted(me, "x", by))
+        pair[0, half] = go(src, dst, p_send.at[0, half], p_recv.at[0, half], sibling)
+
+    def pass_attn(way, by, half):
+        near_a[way, half].wait_recv()
+        block = attn_at(-by, core, half * half_rows, half_rows)
+        if way == half:
+            far_a[way] = go(block, block, f_send.at[way], f_recv.at[way], shifted(me, "x", by))
+        pair[-by, half] = go(block, block, p_send.at[1 + way, half], p_recv.at[1 + way, half], sibling)
+
+    chunks = rows // step
+    for at in range(chunks):
         for load in loads[at]:
             load.wait()
         attend_rows(at * step, step, lengths_ref, query_ref, fresh_key_ref, fresh_value_ref, keys, values, attn_ref)
+        if at == chunks // 2 - 1:
+            send_attn(0)
+    send_attn(1)
     own_a = pltpu.make_async_copy(attn_ref, attn_at(0, core), local_sem.at[1])
     own_a.start()
-    for way, by in ((0, 1), (1, -1)):
-        near_a[way] = go(attn_ref, attn_at(0, core), a_send.at[way], a_recv.at[way], shifted(me, "x", by))
-    pair[0] = go(attn_ref, attn_at(0, core), p_send.at[0], p_recv.at[0], sibling)
     for way, by in ((0, 1), (1, -1)):
         near_w[way].wait_recv()
         block = weight_at(-by, way * half_depth, half_depth)
         far_w[way] = go(block, block, w_send.at[2 + way], w_recv.at[2 + way], shifted(me, "y", by))
-    for way, by in ((0, 1), (1, -1)):
-        near_a[way].wait_recv()
-        block = attn_at(-by, core, way * half_rows, half_rows)
-        far_a[way] = go(block, block, a_send.at[2 + way], a_recv.at[2 + way], shifted(me, "x", by))
-        block = attn_at(-by, core)
-        pair[-by] = go(block, block, p_send.at[1 + way], p_recv.at[1 + way], sibling)
+    for half in (0, 1):
+        for way, by in ((0, 1), (1, -1)):
+            pass_attn(way, by, half)
     for way in (0, 1):
         far_a[way].wait_recv()
-    block = attn_at(2, core)
-    pair[2] = go(block, block, p_send.at[3], p_recv.at[3], sibling)
+        block = attn_at(2, core, way * half_rows, half_rows)
+        pair[2, way] = go(block, block, p_send.at[3, way], p_recv.at[3, way], sibling)
     normed_ref[:, WIDTH : WIDTH + 128] = route_block(names_ref, names_here[...], weights_here[...], table)
     normed_ref[:, WIDTH + 128 :] = jnp.zeros((rows // SIDE, WIDE - WIDTH - 128), normed_ref.dtype)
     own_w.wait()
@@ -232,7 +243,8 @@
     order = (0, 1, -1, 2)
     to_head = {}
     for number, by in enumerate(order):
-        pair[by].wait_recv()
+        for half in (0, 1):
+            pair[by, half].wait_recv()
         at = (me["x"] + by) % SIDE
         block = attn_all[at].reshape(2 * rows, depth)
         part = jnp.dot(block, weight_all[...], preferred_element_type=jnp.float32).astype(jnp.bfloat16)
@@ -316,7 +328,7 @@
             pltpu.VMEM((SIDE, 2, share, width), bf16),
             pltpu.VMEM((SIDE, 2, share, width), bf16),
             dma((3,)), dma((7,)), dma((rows // 16,)), dma((rows // 16,)),
-            dma((4,)), dma((4,)), dma((4,)), dma((4,)), dma((4,)), dma((4,)),
+            dma((4,)), dma((4,)), dma((2, 2)), dma((2, 2)), dma((2,)), dma((2,)), dma((4, 2)), dma((4, 2)),
             dma((4, 3)), dma((4, 3)), dma((4, 2)), dma((4, 2)),
         ],
         compiler_params=pltpu.CompilerParams(collective_id=3, has_side_effects=True, vmem_limit_bytes=60 * 1024 * 1024),
@@ -465,8 +477,8 @@
     send_near(0, 2)
     send_far(1, 1)
     take_far(1, 1)
+    send_far(0, 2)
     send_near(1, 2)
-    send_far(0, 2)
     take_far(0, 2)
     settle(0)
     send_far(1, 2)

time: 175 us -> 168 us (0.960)
  Pallas kernels: 173 us -> 166 us
    pallas_call x1, Pallas kernels: 71 us -> 65.1 us  [gather_and_open(): pl.pallas_call(open_kernel, out_shape=(jax.ShapeDtypeStruct((2, groups *...]
where the time goes in v3:
time: 168 us
  Pallas kernels  166 us (99%)
    pallas_call x1, Pallas kernels, gather_and_open(): pl.pallas_call(open_kernel, out_shape=(jax.ShapeDtypeStruct((2, groups *...  65.1 us
    pallas_call x1, Pallas kernels, close_and_reduce(): pl.pallas_call(close_kernel, out_shape=jax.ShapeDtypeStruct((BLOCK, WIDTH...  60.9 us
    pallas_call x1, Pallas kernels, attend_and_project(): pl.pallas_call(attend_and_project_kernel, out_shape=(jax.ShapeDtypeStruct...  40.4 us

profile of v3, /device:TPU:0, one launch (start us, length us, event | category | flops | bytes accessed | tf_op | source)
XLA Modules:
  0.0 168.1 jit_solution(4668954116475793564)
XLA Ops:
  0.0 40.4 %shard_map.136 = (f32[16,4096]{1,0:T(8,128)}, bf16[16,4352]{1,0:T(8,128)(2,1)}) custom-call(s32[64]{0:T(128)} %lengths_ref.1, s32[8,16]{1,0:T(8,128)} %bitcast.3, bf16[64,2048]{1,0:T(8,128)(2,1)} %query_in.1, bf16[64,128]{1,0:T(8,128)(2,1)} %fresh_key_in.1, bf16[64,128]{1,0:T(8,128)(2,1)} %fresh_value_in.1, bf16[64,1,256,128]{3,2,1,0:T(8,128)(2,1)} %key_ref.1, ...), custom_call_target="tpu_custom_call" | custom-call | tf_op jit(solution)/shard_map/pallas_call | solution.py:304
  40.5 65.1 %shard_map.137 = (bf16[2,512,384]{2,1,0:T(8,128)(2,1)}, bf16[8,256,128]{2,1,0:T(8,128)(2,1)}) custom-call(bf16[16,4352]{1,0:T(8,128)(2,1)} %get-tuple-element.10.mine_ref, bf16[2,4096,384]{2,1,0:T(8,128)(2,1)} %gate_ref.1, bf16[2,4096,384]{2,1,0:T(8,128)(2,1)} %up_ref.1), custom_call_target="tpu_custom_call" | custom-call | tf_op jit(solution)/shard_map/pallas_call | solution.py:503
  105.6 0.0 copy-start
  105.6 60.9 %shard_map.138 = f32[16,4096]{1,0:T(8,128)} custom-call(bf16[2,512,384]{2,1,0:T(8,128)(2,1)} %get-tuple-element.11.act_ref, bf16[8,256,128]{2,1,0:T(8,128)(2,1)} %get-tuple-element.12.pick_ref, bf16[2,384,4096]{2,1,0:T(8,128)(2,1)} %down_ref.1), custom_call_target="tpu_custom_call" | custom-call | tf_op jit(solution)/shard_map/pallas_call | solution.py:699
  166.5 0.0 copy-done
  166.5 1.6 add_convert_fusion
Async XLA Ops:
  105.6 60.9 %copy-start = (f32[16,4096]{1,0:T(8,128)S(1)}, f32[16,4096]{1,0:T(8,128)}, u32[]{:S(2)}) copy-start(f32[16,4096]{1,0:T(8,128)} %get-tuple-element.9) | copy-start | bytes 786436

commit v4 on v3

--- a/solution.py
+++ b/solution.py
@@ -603,8 +603,8 @@
         copy.start()
         near[part, stage, way, half] = copy
 
-    def send_far(wave, stage):
-        for part in range(3 * wave, 3 * wave + 3):
+    def send_far(wave, stage, parts=range(3)):
+        for part in (3 * wave + at for at in parts):
             if stage == 0:
                 add_pair(part, 0, 2)
             for way, by in ((0, 1), (1, -1)):
@@ -615,8 +615,8 @@
                 copy.start()
                 far[part, stage, way] = copy
 
-    def send_near(wave, stage):
-        for part in range(3 * wave, 3 * wave + 3):
+    def send_near(wave, stage, parts=range(3)):
+        for part in (3 * wave + at for at in parts):
             for way, by in ((0, 1), (1, -1)):
                 if stage == 0:
                     add_pair(part, 1 + way, by)
@@ -657,10 +657,14 @@
                     start, size = (start, low) if half == 0 else (start + low, size - low)
                     out_ref[:, pl.ds(start, size)] = total
 
-    for part in range(3):
-        multiply(part)
-    send_far(0, 0)
-    send_near(0, 0)
+    multiply(0)
+    multiply(1)
+    send_far(0, 0, (0,))
+    multiply(2)
+    send_far(0, 0, (1,))
+    send_near(0, 0, (0,))
+    send_far(0, 0, (2,))
+    send_near(0, 0, (1, 2))
     for part in range(3, 6):
         multiply(part)
     relay(0, 0)

time: 168 us -> 169 us (level)
  no operation moved by 1% of the time
where the time goes in v4:
time: 169 us
  Pallas kernels  167 us (99%)
    pallas_call x1, Pallas kernels, gather_and_open(): pl.pallas_call(open_kernel, out_shape=(jax.ShapeDtypeStruct((2, groups *...  65.1 us
    pallas_call x1, Pallas kernels, close_and_reduce(): pl.pallas_call(close_kernel, out_shape=jax.ShapeDtypeStruct((BLOCK, WIDTH...  61.3 us
    pallas_call x1, Pallas kernels, attend_and_project(): pl.pallas_call(attend_and_project_kernel, out_shape=(jax.ShapeDtypeStruct...  40.4 us

profile of v4, /device:TPU:0, one launch (start us, length us, event | category | flops | bytes accessed | tf_op | source)
XLA Modules:
  0.0 168.5 jit_solution(9113531122109773360)
XLA Ops:
  0.0 40.4 %shard_map.136 = (f32[16,4096]{1,0:T(8,128)}, bf16[16,4352]{1,0:T(8,128)(2,1)}) custom-call(s32[64]{0:T(128)} %lengths_ref.1, s32[8,16]{1,0:T(8,128)} %bitcast.3, bf16[64,2048]{1,0:T(8,128)(2,1)} %query_in.1, bf16[64,128]{1,0:T(8,128)(2,1)} %fresh_key_in.1, bf16[64,128]{1,0:T(8,128)(2,1)} %fresh_value_in.1, bf16[64,1,256,128]{3,2,1,0:T(8,128)(2,1)} %key_ref.1, ...), custom_call_target="tpu_custom_call" | custom-call | tf_op jit(solution)/shard_map/pallas_call | solution.py:304
  40.5 65.1 %shard_map.137 = (bf16[2,512,384]{2,1,0:T(8,128)(2,1)}, bf16[8,256,128]{2,1,0:T(8,128)(2,1)}) custom-call(bf16[16,4352]{1,0:T(8,128)(2,1)} %get-tuple-element.10.mine_ref, bf16[2,4096,384]{2,1,0:T(8,128)(2,1)} %gate_ref.1, bf16[2,4096,384]{2,1,0:T(8,128)(2,1)} %up_ref.1), custom_call_target="tpu_custom_call" | custom-call | tf_op jit(solution)/shard_map/pallas_call | solution.py:503
  105.6 0.0 copy-start
  105.6 61.3 %shard_map.138 = f32[16,4096]{1,0:T(8,128)} custom-call(bf16[2,512,384]{2,1,0:T(8,128)(2,1)} %get-tuple-element.11.act_ref, bf16[8,256,128]{2,1,0:T(8,128)(2,1)} %get-tuple-element.12.pick_ref, bf16[2,384,4096]{2,1,0:T(8,128)(2,1)} %down_ref.1), custom_call_target="tpu_custom_call" | custom-call | tf_op jit(solution)/shard_map/pallas_call | solution.py:703
  166.9 0.0 copy-done
  166.9 1.6 add_convert_fusion
Async XLA Ops:
  105.6 61.3 %copy-start = (f32[16,4096]{1,0:T(8,128)S(1)}, f32[16,4096]{1,0:T(8,128)}, u32[]{:S(2)}) copy-start(f32[16,4096]{1,0:T(8,128)} %get-tuple-element.9) | copy-start | bytes 786436
